TPU v7x, 32 devices: a whole 2x2x4 slice. The times are simulated.
32 devices in a mesh: groups: 2 (over y), gx: 4 (over z), gy: 2 (over x), gz: 2 (over core).
Axes of the slice: x: 2, y: 2, z: 4, core: 2. Of those that a mesh axis runs over, the one named last changes fastest.
Arguments:
- fields: float32 [128, 8, 512], P(('groups', 'gx', 'gy', 'gz')), parts along dimension 0, may hold values from -6 to 6
- courants: float32 [128, 3, 512], P(('groups', 'gx', 'gy', 'gz')), parts along dimension 0, may hold values from -0.3 to 0.3, as said below
- bin_moments: bfloat16 [192, 264, 512], P(('groups', 'gx', 'gy', 'gz')), parts along dimension 0, may hold values from -6 to 6
- block_costs: int32 [128], P('groups'), parts along dimension 0, may hold values from 0 to 2, as said below
- block_owner: int32 [128], P('groups'), parts along dimension 0, may hold values from 0 to 3, as said below
- collision: bfloat16 [66, 4356], replicated, may hold values from -0.029907227 to 0.029907227
Outputs:
- fields_out: float32 [128, 8, 512], P(('groups', 'gx', 'gy', 'gz')), parts along dimension 0
- bins_out: bfloat16 [192, 264, 512], P(('groups', 'gx', 'gy', 'gz')), parts along dimension 0
There are 2 independent parts, one for each index of `groups`. A program takes and returns all parts, laid end to end along the dimension named above; an argument that names none is the same for every part. Nothing has to cross between parts.
Inputs may be any that keep to these rules, and one draw needn't show every extreme that they name: `block_owner`: in every column the blocks of each device of gx form one run of consecutive positions, the runs in the order of the devices; each device holds 2 to 6 blocks of a column, and some device holds 6. `block_costs`: the blocks that one device holds in one column need 4 substeps together. `courants`: the first component lies between 0.05 and 0.3.
All inputs are finite; a program needn't handle non-finite values.
Results may differ from a plain program's by a relative error of at most 0.0058.
Values may be sent and summed in bfloat16 or wider, within the bound.
A program may use at most 64 MiB of HBM per device.

v0:
```python
from functools import partial
import math

import jax
import jax.numpy as jnp
from jax import lax
from jax.sharding import PartitionSpec as P

BX = 8
BY = 8
BZ = 8
ITERS = 2


LATENT = 2.5
SAT_SCALE = 0.5
SAT_SLOPE = 0.2
GROWTH_RATE = 0.02
SOLUTE_WEIGHT = 0.5


def with_halo(block, sides, width):
    for axis, dim in sides:
        count = lax.axis_size(axis)
        forward = [(i, i + 1) for i in range(count - 1)]
        backward = [(target, source) for source, target in forward]
        low = lax.ppermute(
            lax.slice_in_dim(block, block.shape[dim] - width, None, axis=dim), axis, forward
        )
        high = lax.ppermute(lax.slice_in_dim(block, 0, width, axis=dim), axis, backward)
        block = jnp.concatenate([low, block, high], axis=dim)
    return block


def passed_along(block, axis, distance):
    devices = range(lax.axis_size(axis))
    route = [(i - distance, i) for i in devices if i - distance in devices]
    return lax.ppermute(block, axis, route)


def upwind(padded, courant):
    centre = padded[:, 1:-1, 1:-1, 1:-1]
    sides = (
        (padded[:, :-2, 1:-1, 1:-1], padded[:, 2:, 1:-1, 1:-1]),
        (padded[:, 1:-1, :-2, 1:-1], padded[:, 1:-1, 2:, 1:-1]),
        (padded[:, 1:-1, 1:-1, :-2], padded[:, 1:-1, 1:-1, 2:]),
    )
    result = centre
    for direction in range(3):
        lower_side, upper_side = sides[direction]
        component = courant[direction]
        result = result - jnp.maximum(component, 0.0) * (centre - lower_side)
        result = result - jnp.minimum(component, 0.0) * (upper_side - centre)
    return result


def to_tile(blocks):
    width = blocks.shape[1]
    shaped = blocks.reshape(2, 2, width, BX, BY, BZ)
    return shaped.transpose(2, 0, 3, 1, 4, 5).reshape(width, 2 * BX, 2 * BY, BZ)


def from_tile(tile_cells):
    width = tile_cells.shape[0]
    shaped = tile_cells.reshape(width, 2, BX, 2, BY, BZ)
    return shaped.transpose(1, 3, 0, 2, 4, 5).reshape(4, width, BX * BY * BZ)


def process(collision, bin_mass, member):
    block_state, inflow, payload, substeps = member
    nbin = collision.shape[0]
    feature_count, block_cells = block_state.shape
    layer_cells = inflow.shape[1]
    moments = block_state.astype(jnp.float32).reshape(
        feature_count, block_cells // layer_cells, layer_cells
    )
    courant = payload[0].reshape(block_cells // layer_cells, layer_cells)
    shifted = jnp.concatenate([inflow.astype(jnp.float32)[:, None, :], moments[:, :-1, :]], axis=1)
    moments = (moments - courant * (moments - shifted)).reshape(feature_count, block_cells)
    number = moments[:nbin]
    mass = moments[nbin : 2 * nbin]
    higher = moments[2 * nbin :]

    def collide(counter, carried):
        count_rows, mass_rows = carried
        products = (
            (count_rows[:, None, :] * count_rows[None, :, :])
            .reshape(nbin * nbin, block_cells)
            .astype(jnp.bfloat16)
        )
        change = jnp.dot(collision, products, preferred_element_type=jnp.float32)
        return (count_rows + change, mass_rows + bin_mass[:, None] * change)

    number, mass = lax.fori_loop(0, substeps, collide, (number, mass))
    excess = payload[1] - SAT_SCALE * jnp.exp(SAT_SLOPE * payload[2])
    growth = GROWTH_RATE * excess[None, :] * (higher[nbin:] + SOLUTE_WEIGHT * higher[:nbin])
    mass = mass + growth
    joined = jnp.concatenate([number, mass, higher], axis=0)
    return (joined.astype(jnp.bfloat16), jnp.sum(growth, axis=0))


def on_device(fields, courants, bin_moments, block_costs, block_owner, collision):
    gx_size = lax.axis_size("gx")
    gx_index = lax.axis_index("gx")
    half_rows = gx_size // 2
    columns = lax.axis_size("gy") * lax.axis_size("gz")
    column = lax.axis_index("gy") * lax.axis_size("gz") + lax.axis_index("gz")
    places = 4 * gx_size
    capacity = bin_moments.shape[0]
    block_cells = bin_moments.shape[2]
    positions = jnp.arange(places, dtype=jnp.int32)
    tile_row = (positions // 4 + half_rows) % gx_size
    column_blocks = (tile_row * columns + column) * 4 + positions % 4
    owners = jnp.take(block_owner, column_blocks)
    column_costs = jnp.take(block_costs, column_blocks)
    device_range = jnp.arange(gx_size, dtype=jnp.int32)
    counts = jnp.sum((owners[:, None] == device_range[None, :]).astype(jnp.int32), axis=0)
    starts = jnp.cumsum(counts) - counts
    own_start = jnp.take(starts, gx_index)
    own_count = jnp.take(counts, gx_index)
    slot_range = jnp.arange(capacity, dtype=jnp.int32)
    slot_valid = slot_range < own_count
    slot_place = jnp.minimum(own_start + slot_range, places - 1)
    slot_cost = jnp.where(slot_valid, jnp.take(column_costs, slot_place), 0)
    live_mask = slot_valid.astype(jnp.float32)
    local_base = 4 * ((gx_index + half_rows) % gx_size)
    local_owner = lax.dynamic_slice_in_dim(owners, local_base, 4)
    nbin = collision.shape[0]
    bin_mass = jnp.exp(jnp.arange(nbin).astype(jnp.float32) * (math.log(8.0) / (nbin - 1)))
    courant_tile = to_tile(courants)
    face_offset = block_cells - BY * BZ
    tile_state = to_tile(fields)
    moment_state = bin_moments
    for iteration in range(ITERS):
        padded = with_halo(tile_state, (("gx", 1), ("gy", 2), ("gz", 3)), 1)
        tile_state = upwind(padded, courant_tile)
        thermo = from_tile(tile_state[0:2])
        payload = jnp.concatenate([courants[:, 0:1], thermo[:, 1:2], thermo[:, 0:1]], axis=1)
        target_mask = (local_owner[None, :] == device_range[:, None]).astype(jnp.float32)
        outgoing = target_mask[:, :, None, None] * payload[None]
        arrived = lax.all_to_all(outgoing, "gx", split_axis=0, concat_axis=0, tiled=True).reshape(
            places, 3, block_cells
        )
        arrived = jnp.roll(arrived.reshape(gx_size, 4, 3, block_cells), -half_rows, axis=0).reshape(
            places, 3, block_cells
        )
        extended = jnp.concatenate(
            [arrived, jnp.zeros((capacity, 3, block_cells), jnp.float32)], axis=0
        )
        slot_load = (
            lax.dynamic_slice_in_dim(extended, own_start, capacity, 0) * live_mask[:, None, None]
        )
        inflow_rows = moment_state[:, :, face_offset:]
        last_two = lax.dynamic_slice_in_dim(inflow_rows, own_count - 2, 2, 0)
        came = passed_along(last_two, "gx", 1)
        inflows = jnp.concatenate([came, inflow_rows[: capacity - 2]], axis=0)
        updated, condensate = lax.map(
            partial(process, collision, bin_mass), (moment_state, inflows, slot_load, slot_cost)
        )
        moment_state = jnp.where(slot_valid[:, None, None], updated, jnp.zeros_like(updated))
        condensate = condensate * live_mask[:, None]
        spread = jnp.zeros((places + capacity, block_cells), jnp.float32)
        spread = lax.dynamic_update_slice_in_dim(spread, condensate, own_start, 0)
        by_tile = jnp.roll(spread[:places].reshape(gx_size, 4, block_cells), -half_rows, axis=0)
        returned = lax.all_to_all(
            by_tile.astype(jnp.bfloat16), "gx", split_axis=0, concat_axis=0, tiled=True
        ).astype(by_tile.dtype)
        gained = jnp.sum(returned, axis=0)
        gained_tile = to_tile(gained[:, None, :])
        tile_state = jnp.concatenate(
            [tile_state[0:1] + LATENT * gained_tile, tile_state[1:2] - gained_tile, tile_state[2:]],
            axis=0,
        )
    return (from_tile(tile_state), moment_state)


def solution(mesh):
    in_specs = (
        P(("groups", "gx", "gy", "gz"), None, None),
        P(("groups", "gx", "gy", "gz"), None, None),
        P(("groups", "gx", "gy", "gz"), None, None),
        P("groups"),
        P("groups"),
        P(),
    )
    out_specs = (
        P(("groups", "gx", "gy", "gz"), None, None),
        P(("groups", "gx", "gy", "gz"), None, None),
    )
    return jax.shard_map(
        on_device, mesh=mesh, in_specs=in_specs, out_specs=out_specs, check_vma=False
    )
```

profile of v0, /device:TPU:12, one launch (start us, length us, event | category | flops | bytes accessed | tf_op | source)
XLA Modules:
  0.0 337.0 jit_solution(12529943399149287768)
XLA Ops:
  4.0 3.5 %collective-permute-start = (f32[8,1,16,8]{2,3,1,0:T(8,128)S(1)}, f32[8,1,16,8]{2,3,1,0:T(8,128)S(1)}, u32[]{:S(2)}, u32[]{:S(2)}) collective-permute-start(f32[8,1,16,8]{2,3,1,0:T(8,128)S(1)} %get-tuple-element.408), channel_id=1, source_target_pairs={{0,4},{4,8},{8,12},{1,5},{5,9},{9,13},{2,6},{6,10},{10,14},{3,7},{... | collective-permute-start | bytes 12296 | tf_op jit(solution)/shard_map/ppermute | solution.py:27
  7.4 2.4 collective-permute-start.1
  9.8 2.8 copy.148
  16.1 3.5 %collective-permute-start.6 = (bf16[2,264,64]{1,2,0:T(8,128)(2,1)}, bf16[2,264,64]{1,2,0:T(8,128)(2,1)}, u32[]{:S(2)}, u32[]{:S(2)}) collective-permute-start(bf16[2,264,64]{1,2,0:T(8,128)(2,1)} %constant_dynamic-slice_fusion.3), channel_id=1, source_target_pairs={{0,4},{4,8},{8,12},{1,5},{5,9},{9,13},{2,6},{6,10},{10,14},{3,7},{... | collective-permute-start | bytes 202760 | tf_op jit(solution)/shard_map/ppermute | solution.py:38
  22.1 2.2 slice_maximum_fusion.2
  27.2 2.1 copy.138
  31.7 5.7 %collective-permute-start.2 = (f32[8,18,1,8]{1,3,2,0:T(8,128)}, f32[8,18,1,8]{1,3,2,0:T(8,128)}, u32[]{:S(2)}, u32[]{:S(2)}) collective-permute-start(f32[8,18,1,8]{1,3,2,0:T(8,128)} %copy.136), channel_id=1, source_target_pairs={{0,2},{1,3},{4,6},{5,7},{8,10},{9,11},{12,14},{13,15},{16,18},{17,... | collective-permute-start | bytes 13832 | tf_op jit(solution)/shard_map/ppermute | solution.py:27
  39.3 2.1 copy.137
  41.4 2.7 pad_maximum_fusion.42
  45.4 4.3 %collective-permute-start.4 = (f32[8,18,18,1]{2,3,1,0:T(1,128)}, f32[8,18,18,1]{2,3,1,0:T(1,128)}, u32[]{:S(2)}, u32[]{:S(2)}) collective-permute-start(f32[8,18,18,1]{2,3,1,0:T(1,128)} %get-tuple-element.395), channel_id=1, source_target_pairs={{0,1},{2,3},{4,5},{6,7},{8,9},{10,11},{12,13},{14,15},{16,17},{18,... | collective-permute-start | bytes 31112 | tf_op jit(solution)/shard_map/ppermute | solution.py:27
  50.9 1.7 min.52
  52.6 1.6 max.38
  54.2 1.7 min.50
  55.9 1.6 max.36
  57.6 1.6 min.48
  59.2 1.6 max.34
  60.9 3.4 %fusion.56 = f32[8,16,16,8]{2,3,1,0:T(8,128)S(1)} fusion(f32[8,16,16,8]{2,3,1,0:T(8,128)} %copy-done.5, f32[8,18,18,1]{2,3,1,0:T(1,128)} %collective-permute-done.5, f32[8,18,1,8]{2,3,1,0:T(8,128)S(1)} %copy.139, f32[8,18,16,8]{2,3,1,0:T(8,128)S(1)} %constant_dynamic-update-slice_fusion, f32[8,18,1,8]{2,3,1,0:T(8,128)} %copy.137, ...), kind=kLoop, calls=%fused_computation.113 | loop fusion | flops 458752 | bytes 292096 | tf_op jit(solution)/shard_map/sub | solution.py:53
  66.5 4.3 %all-to-all-start = ((f32[4,4,3,512]{3,1,2,0:T(4,128)}), f32[4,4,3,512]{3,1,2,0:T(4,128)S(1)}, u32[]{:S(2)}, u32[]{:S(2)}) async-start(f32[4,4,3,512]{3,1,2,0:T(4,128)} %broadcast_multiply_fusion.1), calls=%async_computation | async-start | bytes 196608 | tf_op jit(solution)/shard_map/all_to_all | solution.py:141
  71.9 3.8 %all-to-all-done = f32[4,4,3,512]{3,1,2,0:T(4,128)S(1)} async-done(((f32[4,4,3,512]{3,1,2,0:T(4,128)}), f32[4,4,3,512]{3,1,2,0:T(4,128)S(1)}, u32[]{:S(2)}, u32[]{:S(2)}) %all-to-all-start) | async-done | bytes 98336 | tf_op jit(solution)/shard_map/all_to_all | solution.py:141
  77.2 96.5 %while.55 = (s32[]{:T(128)}, bf16[6,264,512]{2,1,0:T(8,128)(2,1)}, f32[6,512]{1,0:T(8,128)S(1)}, bf16[6,264,512]{1,2,0:T(8,128)(2,1)}, f32[6,3,512]{2,0,1:T(8,12...) while((s32[]{:T(128)}, bf16[6,264,512]{2,1,0:T(8,128)(2,1)}, ...), condition=%wide.region_6.8_spmd.clone, body=%wide.region_2.7_spmd.clone.sunk | while | flops 300733568 | bytes 25449868 | solution.py:157
  81.6 30.8 %while.58 = (s32[]{:T(128)}, f32[66,512]{1,0:T(8,128)S(1)}, f32[66,512]{1,0:T(8,128)S(1)}, s32[]{:T(128)}, bf16[66,4356]{1,0:T(8,128)(2,1)S(1)}, /*index=5*/f32[66]{0:T(128)S(1)}, s32[]{:T(128)}) while((s32[]{:T(128)}, f32[66,512]{1,0:T(8,128)S(1)}, f32[66,512]{1,0:T(8,128)S(1)}, s32[]{:T(128)}, bf16[66,4356]{1,0:T(8,128)(2,1)S(1)}, ...), condition=%wide.region_4.5_spmd, body=%wide.region_3.4_spmd.sunk | while | flops 298957824 | bytes 19093348 | solution.py:94
  82.2 3.7 %multiply_convert_fusion.5 = bf16[66,66,512]{2,1,0:T(8,128)(2,1)} fusion(f32[66,512]{1,0:T(8,128)S(1)} %get-tuple-element.710), kind=kLoop, calls=%fused_computation.5.clone.1 | loop fusion | flops 4460544 | bytes 4595712 | tf_op jit(solution)/shard_map/while/body/eval_jaxpr/while/body/convert_element_type | solution.py:89
  85.9 7.5 %convert_element_type.145 = bf16[4356,512]{1,0:T(8,128)(2,1)} reshape(bf16[66,66,512]{2,1,0:T(8,128)(2,1)} %multiply_convert_fusion.5) | data formatting | bytes 8921088 | tf_op jit(solution)/shard_map/while/body/eval_jaxpr/while/body/convert_element_type | solution.py:89
  93.4 3.2 multiply_add_fusion.5
  97.3 3.7 %multiply_convert_fusion.5 = bf16[66,66,512]{2,1,0:T(8,128)(2,1)} fusion(f32[66,512]{1,0:T(8,128)S(1)} %get-tuple-element.710), kind=kLoop, calls=%fused_computation.5.clone.1 | loop fusion | flops 4460544 | bytes 4595712 | tf_op jit(solution)/shard_map/while/body/eval_jaxpr/while/body/convert_element_type | solution.py:89
  100.9 7.5 %convert_element_type.145 = bf16[4356,512]{1,0:T(8,128)(2,1)} reshape(bf16[66,66,512]{2,1,0:T(8,128)(2,1)} %multiply_convert_fusion.5) | data formatting | bytes 8921088 | tf_op jit(solution)/shard_map/while/body/eval_jaxpr/while/body/convert_element_type | solution.py:89
  108.5 3.2 multiply_add_fusion.5
  117.7 30.8 %while.58 = (s32[]{:T(128)}, f32[66,512]{1,0:T(8,128)S(1)}, f32[66,512]{1,0:T(8,128)S(1)}, s32[]{:T(128)}, bf16[66,4356]{1,0:T(8,128)(2,1)S(1)}, /*index=5*/f32[66]{0:T(128)S(1)}, s32[]{:T(128)}) while((s32[]{:T(128)}, f32[66,512]{1,0:T(8,128)S(1)}, f32[66,512]{1,0:T(8,128)S(1)}, s32[]{:T(128)}, bf16[66,4356]{1,0:T(8,128)(2,1)S(1)}, ...), condition=%wide.region_4.5_spmd, body=%wide.region_3.4_spmd.sunk | while | flops 298957824 | bytes 19093348 | solution.py:94
  118.3 3.7 %multiply_convert_fusion.5 = bf16[66,66,512]{2,1,0:T(8,128)(2,1)} fusion(f32[66,512]{1,0:T(8,128)S(1)} %get-tuple-element.710), kind=kLoop, calls=%fused_computation.5.clone.1 | loop fusion | flops 4460544 | bytes 4595712 | tf_op jit(solution)/shard_map/while/body/eval_jaxpr/while/body/convert_element_type | solution.py:89
  122.0 7.5 %convert_element_type.145 = bf16[4356,512]{1,0:T(8,128)(2,1)} reshape(bf16[66,66,512]{2,1,0:T(8,128)(2,1)} %multiply_convert_fusion.5) | data formatting | bytes 8921088 | tf_op jit(solution)/shard_map/while/body/eval_jaxpr/while/body/convert_element_type | solution.py:89
  129.6 3.2 multiply_add_fusion.5
  133.4 3.7 %multiply_convert_fusion.5 = bf16[66,66,512]{2,1,0:T(8,128)(2,1)} fusion(f32[66,512]{1,0:T(8,128)S(1)} %get-tuple-element.710), kind=kLoop, calls=%fused_computation.5.clone.1 | loop fusion | flops 4460544 | bytes 4595712 | tf_op jit(solution)/shard_map/while/body/eval_jaxpr/while/body/convert_element_type | solution.py:89
  137.1 7.5 %convert_element_type.145 = bf16[4356,512]{1,0:T(8,128)(2,1)} reshape(bf16[66,66,512]{2,1,0:T(8,128)(2,1)} %multiply_convert_fusion.5) | data formatting | bytes 8921088 | tf_op jit(solution)/shard_map/while/body/eval_jaxpr/while/body/convert_element_type | solution.py:89
  144.6 3.2 multiply_add_fusion.5
  174.5 4.1 %all-to-all-start.1 = ((bf16[4,4,512]{2,1,0:T(4,128)(2,1)}), bf16[4,4,512]{2,1,0:T(4,128)(2,1)S(1)}, u32[]{:S(2)}, u32[]{:S(2)}) async-start(bf16[4,4,512]{2,1,0:T(4,128)(2,1)} %pad_maximum_fusion.45), calls=%async_computation.1 | async-start | bytes 32768 | tf_op jit(solution)/shard_map/all_to_all | solution.py:165
  178.7 4.2 %all-to-all-done.1 = bf16[4,4,512]{2,1,0:T(4,128)(2,1)S(1)} async-done(((bf16[4,4,512]{2,1,0:T(4,128)(2,1)}), bf16[4,4,512]{2,1,0:T(4,128)(2,1)S(1)}, u32[]{:S(2)}, u32[]{:S(2)}) %all-to-all-start.1) | async-done | bytes 16416 | tf_op jit(solution)/shard_map/all_to_all | solution.py:165
  183.3 3.3 collective-permute-start.8
  186.6 2.6 collective-permute-start.7
  189.8 2.7 collective-permute-done.7
  193.5 1.5 copy.153
  196.8 4.5 %collective-permute-start.9 = (f32[8,18,1,8]{1,3,2,0:T(8,128)S(1)}, f32[8,18,1,8]{1,3,2,0:T(8,128)S(1)}, u32[]{:S(2)}, u32[]{:S(2)}) collective-permute-start(f32[8,18,1,8]{1,3,2,0:T(8,128)S(1)} %copy.151), channel_id=1, source_target_pairs={{0,2},{1,3},{4,6},{5,7},{8,10},{9,11},{12,14},{13,15},{16,18},{17,... | collective-permute-start | bytes 13832 | tf_op jit(solution)/shard_map/ppermute | solution.py:27
  201.3 2.0 broadcast_select_fusion.1
  207.6 3.0 collective-permute-start.11
  211.3 2.7 collective-permute-start.13
  214.1 1.9 fusion.31
  217.4 5.3 %all-to-all-start.2 = ((f32[4,4,3,512]{3,1,2,0:T(4,128)}), f32[4,4,3,512]{3,1,2,0:T(4,128)S(1)}, u32[]{:S(2)}, u32[]{:S(2)}) async-start(f32[4,4,3,512]{3,1,2,0:T(4,128)} %broadcast_multiply_fusion), calls=%async_computation.2 | async-start | bytes 196608 | tf_op jit(solution)/shard_map/all_to_all | solution.py:141
  225.0 2.5 all-to-all-done.2
  229.0 96.0 %while.57 = (s32[]{:T(128)}, bf16[6,264,512]{2,1,0:T(8,128)(2,1)}, f32[6,512]{1,0:T(8,128)S(1)}, bf16[6,264,512]{2,1,0:T(8,128)(2,1)}, f32[6,3,512]{2,0,1:T(8,12...) while((s32[]{:T(128)}, bf16[6,264,512]{2,1,0:T(8,128)(2,1)}, ...), condition=%wide.region_12.14_spmd.clone, body=%wide.region_8.13_spmd.clone.sunk | while | flops 300733568 | bytes 25990532 | solution.py:157
  233.4 30.6 %while.59 = (s32[]{:T(128)}, f32[66,512]{1,0:T(8,128)S(1)}, f32[66,512]{1,0:T(8,128)S(1)}, s32[]{:T(128)}, bf16[66,4356]{1,0:T(8,128)(2,1)S(1)}, /*index=5*/f32[66]{0:T(128)S(1)}, s32[]{:T(128)}) while((s32[]{:T(128)}, f32[66,512]{1,0:T(8,128)S(1)}, f32[66,512]{1,0:T(8,128)S(1)}, s32[]{:T(128)}, bf16[66,4356]{1,0:T(8,128)(2,1)S(1)}, ...), condition=%wide.region_10.11_spmd, body=%wide.region_9.10_spmd.sunk | while | flops 298957824 | bytes 19093348 | solution.py:94
  233.9 3.7 %multiply_convert_fusion.4 = bf16[66,66,512]{2,1,0:T(8,128)(2,1)} fusion(f32[66,512]{1,0:T(8,128)S(1)} %get-tuple-element.689), kind=kLoop, calls=%fused_computation.8.clone.1 | loop fusion | flops 4460544 | bytes 4595712 | tf_op jit(solution)/shard_map/while/body/eval_jaxpr/while/body/convert_element_type | solution.py:89
  237.6 7.5 %convert_element_type.143 = bf16[4356,512]{1,0:T(8,128)(2,1)} reshape(bf16[66,66,512]{2,1,0:T(8,128)(2,1)} %multiply_convert_fusion.4) | data formatting | bytes 8921088 | tf_op jit(solution)/shard_map/while/body/eval_jaxpr/while/body/convert_element_type | solution.py:89
  245.1 3.2 multiply_add_fusion.4
  248.9 3.7 %multiply_convert_fusion.4 = bf16[66,66,512]{2,1,0:T(8,128)(2,1)} fusion(f32[66,512]{1,0:T(8,128)S(1)} %get-tuple-element.689), kind=kLoop, calls=%fused_computation.8.clone.1 | loop fusion | flops 4460544 | bytes 4595712 | tf_op jit(solution)/shard_map/while/body/eval_jaxpr/while/body/convert_element_type | solution.py:89
  252.6 7.5 %convert_element_type.143 = bf16[4356,512]{1,0:T(8,128)(2,1)} reshape(bf16[66,66,512]{2,1,0:T(8,128)(2,1)} %multiply_convert_fusion.4) | data formatting | bytes 8921088 | tf_op jit(solution)/shard_map/while/body/eval_jaxpr/while/body/convert_element_type | solution.py:89
  260.1 3.2 multiply_add_fusion.4
  269.4 30.6 %while.59 = (s32[]{:T(128)}, f32[66,512]{1,0:T(8,128)S(1)}, f32[66,512]{1,0:T(8,128)S(1)}, s32[]{:T(128)}, bf16[66,4356]{1,0:T(8,128)(2,1)S(1)}, /*index=5*/f32[66]{0:T(128)S(1)}, s32[]{:T(128)}) while((s32[]{:T(128)}, f32[66,512]{1,0:T(8,128)S(1)}, f32[66,512]{1,0:T(8,128)S(1)}, s32[]{:T(128)}, bf16[66,4356]{1,0:T(8,128)(2,1)S(1)}, ...), condition=%wide.region_10.11_spmd, body=%wide.region_9.10_spmd.sunk | while | flops 298957824 | bytes 19093348 | solution.py:94
  269.9 3.7 %multiply_convert_fusion.4 = bf16[66,66,512]{2,1,0:T(8,128)(2,1)} fusion(f32[66,512]{1,0:T(8,128)S(1)} %get-tuple-element.689), kind=kLoop, calls=%fused_computation.8.clone.1 | loop fusion | flops 4460544 | bytes 4595712 | tf_op jit(solution)/shard_map/while/body/eval_jaxpr/while/body/convert_element_type | solution.py:89
  273.6 7.5 %convert_element_type.143 = bf16[4356,512]{1,0:T(8,128)(2,1)} reshape(bf16[66,66,512]{2,1,0:T(8,128)(2,1)} %multiply_convert_fusion.4) | data formatting | bytes 8921088 | tf_op jit(solution)/shard_map/while/body/eval_jaxpr/while/body/convert_element_type | solution.py:89
  281.2 3.2 multiply_add_fusion.4
  284.9 3.7 %multiply_convert_fusion.4 = bf16[66,66,512]{2,1,0:T(8,128)(2,1)} fusion(f32[66,512]{1,0:T(8,128)S(1)} %get-tuple-element.689), kind=kLoop, calls=%fused_computation.8.clone.1 | loop fusion | flops 4460544 | bytes 4595712 | tf_op jit(solution)/shard_map/while/body/eval_jaxpr/while/body/convert_element_type | solution.py:89
  288.6 7.5 %convert_element_type.143 = bf16[4356,512]{1,0:T(8,128)(2,1)} reshape(bf16[66,66,512]{2,1,0:T(8,128)(2,1)} %multiply_convert_fusion.4) | data formatting | bytes 8921088 | tf_op jit(solution)/shard_map/while/body/eval_jaxpr/while/body/convert_element_type | solution.py:89
  296.1 3.2 multiply_add_fusion.4
  325.9 4.1 %all-to-all-start.3 = ((bf16[4,4,512]{2,1,0:T(4,128)(2,1)}), bf16[4,4,512]{2,1,0:T(4,128)(2,1)S(1)}, u32[]{:S(2)}, u32[]{:S(2)}) async-start(bf16[4,4,512]{2,1,0:T(4,128)(2,1)} %pad_maximum_fusion.46), calls=%async_computation.3 | async-start | bytes 32768 | tf_op jit(solution)/shard_map/all_to_all | solution.py:165
  330.1 2.8 broadcast_select_fusion
  (440 shorter events, 110.5 us)
Async XLA Ops:
  0.6 12.1 %copy-start = (s32[64]{0:T(128)S(1)}, s32[64]{0:T(128)}, u32[]{:S(2)}) copy-start(s32[64]{0:T(128)} %param.19) | copy-start | bytes 772
  3.3 21.7 %copy-start.5 = (f32[8,16,16,8]{2,3,1,0:T(8,128)}, f32[8,16,16,8]{2,3,1,0:T(8,128)S(1)}, u32[]{:S(2)}) copy-start(f32[8,16,16,8]{2,3,1,0:T(8,128)S(1)} %reshape.459) | copy-start | bytes 196612
  4.0 21.0 %collective-permute-start = (f32[8,1,16,8]{2,3,1,0:T(8,128)S(1)}, f32[8,1,16,8]{2,3,1,0:T(8,128)S(1)}, u32[]{:S(2)}, u32[]{:S(2)}) collective-permute-start(f32[8,1,16,8]{2,3,1,0:T(8,128)S(1)} %get-tuple-element.408), channel_id=1, source_target_pairs={{0,4},{4,8},{8,12},{1,5},{5,9},{9,13},{2,6},{6,10},{10,14},{3,7},{... | collective-permute-start | bytes 12296 | tf_op jit(solution)/shard_map/ppermute | solution.py:27
  7.4 17.6 %collective-permute-start.1 = (f32[8,1,16,8]{2,3,1,0:T(8,128)}, f32[8,1,16,8]{2,3,1,0:T(8,128)S(1)}, u32[]{:S(2)}, u32[]{:S(2)}) collective-permute-start(f32[8,1,16,8]{2,3,1,0:T(8,128)} %get-tuple-element.407), channel_id=1, source_target_pairs={{4,0},{8,4},{12,8},{5,1},{9,5},{13,9},{6,2},{10,6},{14,10},{7,3},{... | collective-permute-start | bytes 12296 | tf_op jit(solution)/shard_map/ppermute | solution.py:30
  9.8 3.6 %copy-start.2 = (s32[64]{0:T(128)S(1)}, s32[64]{0:T(128)}, u32[]{:S(2)}) copy-start(s32[64]{0:T(128)} %param.20) | copy-start | bytes 772
  12.7 58.1 %copy-start.3 = (bf16[6,264,512]{1,2,0:T(8,128)(2,1)}, bf16[6,264,512]{1,2,0:T(8,128)(2,1)S(1)}, u32[]{:S(2)}) copy-start(bf16[6,264,512]{1,2,0:T(8,128)(2,1)S(1)} %copy.148) | copy-start | bytes 4866052
  12.7 8.3 %copy-start.20 = (f32[4,3,512]{2,0,1:T(4,128)S(1)}, f32[4,3,512]{2,0,1:T(4,128)}, u32[]{:S(2)}) copy-start(f32[4,3,512]{2,0,1:T(4,128)} %param.17) | copy-start | bytes 73732
  16.1 54.8 %collective-permute-start.6 = (bf16[2,264,64]{1,2,0:T(8,128)(2,1)}, bf16[2,264,64]{1,2,0:T(8,128)(2,1)}, u32[]{:S(2)}, u32[]{:S(2)}) collective-permute-start(bf16[2,264,64]{1,2,0:T(8,128)(2,1)} %constant_dynamic-slice_fusion.3), channel_id=1, source_target_pairs={{0,4},{4,8},{8,12},{1,5},{5,9},{9,13},{2,6},{6,10},{10,14},{3,7},{... | collective-permute-start | bytes 202760 | tf_op jit(solution)/shard_map/ppermute | solution.py:38
  25.0 0.6 copy-start.16
  25.6 0.6 copy-start.17
  29.3 8.8 %collective-permute-start.3 = (f32[8,18,1,8]{1,3,2,0:T(8,128)}, f32[8,18,1,8]{1,3,2,0:T(8,128)}, u32[]{:S(2)}, u32[]{:S(2)}) collective-permute-start(f32[8,18,1,8]{1,3,2,0:T(8,128)} %copy.138), channel_id=1, source_target_pairs={{2,0},{3,1},{6,4},{7,5},{10,8},{11,9},{14,12},{15,13},{18,16},{19,... | collective-permute-start | bytes 13832 | tf_op jit(solution)/shard_map/ppermute | solution.py:30
  31.7 7.6 %collective-permute-start.2 = (f32[8,18,1,8]{1,3,2,0:T(8,128)}, f32[8,18,1,8]{1,3,2,0:T(8,128)}, u32[]{:S(2)}, u32[]{:S(2)}) collective-permute-start(f32[8,18,1,8]{1,3,2,0:T(8,128)} %copy.136), channel_id=1, source_target_pairs={{0,2},{1,3},{4,6},{5,7},{8,10},{9,11},{12,14},{13,15},{16,18},{17,... | collective-permute-start | bytes 13832 | tf_op jit(solution)/shard_map/ppermute | solution.py:27
  44.1 16.8 %collective-permute-start.5 = (f32[8,18,18,1]{2,3,1,0:T(1,128)}, f32[8,18,18,1]{2,3,1,0:T(1,128)}, u32[]{:S(2)}, u32[]{:S(2)}) collective-permute-start(f32[8,18,18,1]{2,3,1,0:T(1,128)} %get-tuple-element.396), channel_id=1, source_target_pairs={{1,0},{3,2},{5,4},{7,6},{9,8},{11,10},{13,12},{15,14},{17,16},{19,... | collective-permute-start | bytes 31112 | tf_op jit(solution)/shard_map/ppermute | solution.py:30
  45.4 15.5 %collective-permute-start.4 = (f32[8,18,18,1]{2,3,1,0:T(1,128)}, f32[8,18,18,1]{2,3,1,0:T(1,128)}, u32[]{:S(2)}, u32[]{:S(2)}) collective-permute-start(f32[8,18,18,1]{2,3,1,0:T(1,128)} %get-tuple-element.395), channel_id=1, source_target_pairs={{0,1},{2,3},{4,5},{6,7},{8,9},{10,11},{12,13},{14,15},{16,17},{18,... | collective-permute-start | bytes 31112 | tf_op jit(solution)/shard_map/ppermute | solution.py:27
  50.9 14.7 %copy-start.18 = (f32[4,1,512]{2,1,0:T(1,128)}, f32[4,1,512]{2,1,0:T(1,128)S(1)}, u32[]{:S(2)}) copy-start(f32[4,1,512]{2,1,0:T(1,128)S(1)} %copy.176) | copy-start | bytes 24580
  60.8 4.9 %copy-start.21 = (f32[4,4]{1,0:T(4,128)S(1)}, f32[4,4]{1,0:T(4,128)}, u32[]{:S(2)}) copy-start(f32[4,4]{1,0:T(4,128)} %fusion.76) | copy-start | bytes 196
  64.3 0.8 copy-start.8
  66.5 9.2 %all-to-all-start = ((f32[4,4,3,512]{3,1,2,0:T(4,128)}), f32[4,4,3,512]{3,1,2,0:T(4,128)S(1)}, u32[]{:S(2)}, u32[]{:S(2)}) async-start(f32[4,4,3,512]{3,1,2,0:T(4,128)} %broadcast_multiply_fusion.1), calls=%async_computation | async-start | bytes 196608 | tf_op jit(solution)/shard_map/all_to_all | solution.py:141
  70.8 6.3 %copy-start.23 = (f32[6]{0:T(128)}, f32[6]{0:T(128)S(1)}, u32[]{:S(2)}) copy-start(f32[6]{0:T(128)S(1)} %fusion.85) | copy-start | bytes 76
  70.8 6.3 %copy-start.1 = (bf16[66,4356]{1,0:T(8,128)(2,1)S(1)}, bf16[66,4356]{1,0:T(8,128)(2,1)}, u32[]{:S(2)}) copy-start(bf16[66,4356]{1,0:T(8,128)(2,1)} %param.21) | copy-start | bytes 1724980
  70.9 6.3 %copy-start.27 = (s32[6]{0:T(128)S(1)}, s32[6]{0:T(128)}, u32[]{:S(2)}) copy-start(s32[6]{0:T(128)} %fusion.82) | copy-start | bytes 76
  77.2 96.5 %copy-start.24 = (f32[6]{0:T(128)S(1)}, f32[6]{0:T(128)}, u32[]{:S(2)}) copy-start(f32[6]{0:T(128)} %copy-done.23) | copy-start | bytes 76
  77.2 101.5 %copy-start.9 = (f32[8,16,16,8]{2,3,1,0:T(8,128)S(1)}, f32[8,16,16,8]{2,3,1,0:T(8,128)}, u32[]{:S(2)}) copy-start(f32[8,16,16,8]{2,3,1,0:T(8,128)} %copy-done.8) | copy-start | bytes 196612
  174.5 8.4 %all-to-all-start.1 = ((bf16[4,4,512]{2,1,0:T(4,128)(2,1)}), bf16[4,4,512]{2,1,0:T(4,128)(2,1)S(1)}, u32[]{:S(2)}, u32[]{:S(2)}) async-start(bf16[4,4,512]{2,1,0:T(4,128)(2,1)} %pad_maximum_fusion.45), calls=%async_computation.1 | async-start | bytes 32768 | tf_op jit(solution)/shard_map/all_to_all | solution.py:165
  183.3 6.4 %collective-permute-start.8 = (f32[8,1,16,8]{2,3,1,0:T(8,128)S(1)}, f32[8,1,16,8]{2,3,1,0:T(8,128)S(1)}, u32[]{:S(2)}, u32[]{:S(2)}) collective-permute-start(f32[8,1,16,8]{2,3,1,0:T(8,128)S(1)} %get-tuple-element.406), channel_id=1, source_target_pairs={{4,0},{8,4},{12,8},{5,1},{9,5},{13,9},{6,2},{10,6},{14,10},{7,3},{... | collective-permute-start | bytes 12296 | tf_op jit(solution)/shard_map/ppermute | solution.py:30
  186.6 5.8 %collective-permute-start.7 = (f32[8,1,16,8]{2,3,1,0:T(8,128)S(1)}, f32[8,1,16,8]{2,3,1,0:T(8,128)S(1)}, u32[]{:S(2)}, u32[]{:S(2)}) collective-permute-start(f32[8,1,16,8]{2,3,1,0:T(8,128)S(1)} %get-tuple-element.405), channel_id=1, source_target_pairs={{0,4},{4,8},{8,12},{1,5},{5,9},{9,13},{2,6},{6,10},{10,14},{3,7},{... | collective-permute-start | bytes 12296 | tf_op jit(solution)/shard_map/ppermute | solution.py:27
  192.5 8.8 %copy-start.4 = (bf16[6,264,512]{2,1,0:T(8,128)(2,1)S(1)}, bf16[6,264,512]{2,1,0:T(8,128)(2,1)}, u32[]{:S(2)}) copy-start(bf16[6,264,512]{2,1,0:T(8,128)(2,1)} %get-tuple-element.808) | copy-start | bytes 4866052
  195.0 9.6 %collective-permute-start.10 = (f32[8,18,1,8]{1,3,2,0:T(8,128)S(1)}, f32[8,18,1,8]{1,3,2,0:T(8,128)S(1)}, u32[]{:S(2)}, u32[]{:S(2)}) collective-permute-start(f32[8,18,1,8]{1,3,2,0:T(8,128)S(1)} %copy.153), channel_id=1, source_target_pairs={{2,0},{3,1},{6,4},{7,5},{10,8},{11,9},{14,12},{15,13},{18,16},{19,... | collective-permute-start | bytes 13832 | tf_op jit(solution)/shard_map/ppermute | solution.py:30
  196.8 8.3 %collective-permute-start.9 = (f32[8,18,1,8]{1,3,2,0:T(8,128)S(1)}, f32[8,18,1,8]{1,3,2,0:T(8,128)S(1)}, u32[]{:S(2)}, u32[]{:S(2)}) collective-permute-start(f32[8,18,1,8]{1,3,2,0:T(8,128)S(1)} %copy.151), channel_id=1, source_target_pairs={{0,2},{1,3},{4,6},{5,7},{8,10},{9,11},{12,14},{13,15},{16,18},{17,... | collective-permute-start | bytes 13832 | tf_op jit(solution)/shard_map/ppermute | solution.py:27
  204.5 9.5 %copy-start.10 = (f32[16,16,8]{1,2,0:T(8,128)S(1)}, f32[16,16,8]{1,2,0:T(8,128)}, u32[]{:S(2)}) copy-start(f32[16,16,8]{1,2,0:T(8,128)} %min.52) | copy-start | bytes 24580
  204.5 9.5 %copy-start.11 = (f32[16,16,8]{1,2,0:T(8,128)S(1)}, f32[16,16,8]{1,2,0:T(8,128)}, u32[]{:S(2)}) copy-start(f32[16,16,8]{1,2,0:T(8,128)} %max.38) | copy-start | bytes 24580
  204.5 9.5 %copy-start.12 = (f32[16,16,8]{1,2,0:T(8,128)S(1)}, f32[16,16,8]{1,2,0:T(8,128)}, u32[]{:S(2)}) copy-start(f32[16,16,8]{1,2,0:T(8,128)} %min.50) | copy-start | bytes 24580
  204.6 9.5 %copy-start.13 = (f32[16,16,8]{1,2,0:T(8,128)S(1)}, f32[16,16,8]{1,2,0:T(8,128)}, u32[]{:S(2)}) copy-start(f32[16,16,8]{1,2,0:T(8,128)} %max.36) | copy-start | bytes 24580
  204.6 9.5 %copy-start.14 = (f32[16,16,8]{1,2,0:T(8,128)S(1)}, f32[16,16,8]{1,2,0:T(8,128)}, u32[]{:S(2)}) copy-start(f32[16,16,8]{1,2,0:T(8,128)} %min.48) | copy-start | bytes 24580
  204.6 9.5 %copy-start.15 = (f32[16,16,8]{1,2,0:T(8,128)S(1)}, f32[16,16,8]{1,2,0:T(8,128)}, u32[]{:S(2)}) copy-start(f32[16,16,8]{1,2,0:T(8,128)} %max.34) | copy-start | bytes 24580
  206.3 7.7 %collective-permute-start.12 = (f32[8,18,18,1]{2,3,1,0:T(1,128)S(1)}, f32[8,18,18,1]{2,3,1,0:T(1,128)S(1)}, u32[]{:S(2)}, u32[]{:S(2)}) collective-permute-start(f32[8,18,18,1]{2,3,1,0:T(1,128)S(1)} %get-tuple-element.394), channel_id=1, source_target_pairs={{1,0},{3,2},{5,4},{7,6},{9,8},{11,10},{13,12},{15,14},{17,16},{19,... | collective-permute-start | bytes 31112 | tf_op jit(solution)/shard_map/ppermute | solution.py:30
  207.6 6.4 %collective-permute-start.11 = (f32[8,18,18,1]{2,3,1,0:T(1,128)S(1)}, f32[8,18,18,1]{2,3,1,0:T(1,128)S(1)}, u32[]{:S(2)}, u32[]{:S(2)}) collective-permute-start(f32[8,18,18,1]{2,3,1,0:T(1,128)S(1)} %get-tuple-element.393), channel_id=1, source_target_pairs={{0,1},{2,3},{4,5},{6,7},{8,9},{10,11},{12,13},{14,15},{16,17},{18,... | collective-permute-start | bytes 31112 | tf_op jit(solution)/shard_map/ppermute | solution.py:27
  211.3 5.3 %copy-start.19 = (f32[4,1,512]{2,1,0:T(1,128)S(1)}, f32[4,1,512]{2,1,0:T(1,128)}, u32[]{:S(2)}) copy-start(f32[4,1,512]{2,1,0:T(1,128)} %copy-done.18) | copy-start | bytes 24580
  211.3 5.3 %copy-start.22 = (f32[4,4]{1,0:T(4,128)S(1)}, f32[4,4]{1,0:T(4,128)}, u32[]{:S(2)}) copy-start(f32[4,4]{1,0:T(4,128)} %fusion.76) | copy-start | bytes 196
  211.3 12.4 %collective-permute-start.13 = (bf16[2,264,64]{2,1,0:T(8,128)(2,1)}, bf16[2,264,64]{2,1,0:T(8,128)(2,1)}, u32[]{:S(2)}, u32[]{:S(2)}) collective-permute-start(bf16[2,264,64]{2,1,0:T(8,128)(2,1)} %constant_dynamic-slice_fusion.2), channel_id=1, source_target_pairs={{0,4},{4,8},{8,12},{1,5},{5,9},{9,13},{2,6},{6,10},{10,14},{3,7},{... | collective-permute-start | bytes 202760 | tf_op jit(solution)/shard_map/ppermute | solution.py:38
  216.0 7.7 %copy-start.6 = (f32[8,16,16,8]{2,3,1,0:T(8,128)}, f32[8,16,16,8]{2,3,1,0:T(8,128)S(1)}, u32[]{:S(2)}) copy-start(f32[8,16,16,8]{2,3,1,0:T(8,128)S(1)} %fusion.31) | copy-start | bytes 196612
  217.4 10.2 %all-to-all-start.2 = ((f32[4,4,3,512]{3,1,2,0:T(4,128)}), f32[4,4,3,512]{3,1,2,0:T(4,128)S(1)}, u32[]{:S(2)}, u32[]{:S(2)}) async-start(f32[4,4,3,512]{3,1,2,0:T(4,128)} %broadcast_multiply_fusion), calls=%async_computation.2 | async-start | bytes 196608 | tf_op jit(solution)/shard_map/all_to_all | solution.py:141
  224.7 4.2 %copy-start.28 = (s32[6]{0:T(128)S(1)}, s32[6]{0:T(128)}, u32[]{:S(2)}) copy-start(s32[6]{0:T(128)} %fusion.82) | copy-start | bytes 76
  229.0 96.1 %copy-start.25 = (f32[6]{0:T(128)S(1)}, f32[6]{0:T(128)}, u32[]{:S(2)}) copy-start(f32[6]{0:T(128)} %copy-done.23) | copy-start | bytes 76
  229.0 101.1 %copy-start.26 = (pred[6]{0:T(512)(128)(4,1)S(1)}, pred[6]{0:T(512)(128)(4,1)}, u32[]{:S(2)}) copy-start(pred[6]{0:T(512)(128)(4,1)} %iota_compare_fusion.2) | copy-start | bytes 22
  325.9 8.4 %all-to-all-start.3 = ((bf16[4,4,512]{2,1,0:T(4,128)(2,1)}), bf16[4,4,512]{2,1,0:T(4,128)(2,1)S(1)}, u32[]{:S(2)}, u32[]{:S(2)}) async-start(bf16[4,4,512]{2,1,0:T(4,128)(2,1)} %pad_maximum_fusion.46), calls=%async_computation.3 | async-start | bytes 32768 | tf_op jit(solution)/shard_map/all_to_all | solution.py:165
  330.1 4.6 %copy-start.7 = (f32[8,16,16,8]{2,3,1,0:T(8,128)S(1)}, f32[8,16,16,8]{2,3,1,0:T(8,128)}, u32[]{:S(2)}) copy-start(f32[8,16,16,8]{2,3,1,0:T(8,128)} %copy-done.6) | copy-start | bytes 196612
  330.1 4.6 %slice-start = ((f32[8,16,16,8]{2,3,1,0:T(8,128)}), f32[6,16,16,8]{2,3,1,0:T(8,128)S(1)}, s32[]{:S(2)}) async-start(f32[8,16,16,8]{2,3,1,0:T(8,128)} %copy-done.6), calls=%async_computation.4 | async-start | bytes 786432 | tf_op jit(solution)/shard_map/slice | solution.py:171
where the time goes:
time: 343 us; the launch traced here: 337 us
  local copies, waits for them, and re-layouts  144 us (42%)
  other arithmetic  78.2 us (23%)
  starting transfers between devices  58.4 us (17%)
  matrix products  25.7 us (7%)
  waiting for transfers between devices  14.6 us (4%)
  loops' own time  13.2 us (4%)
    convert_element_type x8, local copies, waits for them, and re-layouts, collide(): products = (count_rows[:, None, :] * count_rows[None, :, :]).reshape(nbin...  60.2 us
    convert_element_type x8, other arithmetic, collide(): products = (count_rows[:, None, :] * count_rows[None, :, :]).reshape(nbin...  29.5 us
    dot_general x8, matrix products, collide(): change = jnp.dot(collision, products, preferred_element_type=jnp.float32)  25.7 us
    ppermute x6, starting transfers between devices, with_halo(): lax.ppermute(lax.slice_in_dim(block, block.shape[dim] - width, None, axis...  23.6 us
    dynamic_slice x30, local copies, waits for them, and re-layouts, on_device(): lax.map(partial(process, collision, bin_mass), (moment_state, inflows, sl...  20.5 us
    another operation x12, loops' own time, process(): number, mass = lax.fori_loop(0, substeps, collide, (number, mass))  12.1 us
    ppermute x6, starting transfers between devices, with_halo(): lax.ppermute(lax.slice_in_dim(block, 0, width, axis=dim), axis, backward)  10.8 us
    all_to_all x2, starting transfers between devices, on_device(): lax.all_to_all(outgoing, 'gx', split_axis=0, concat_axis=0, tiled=True)  9.61 us
  transfers between devices with their start and end apart: 18, of which 5 were waited for; matrix products, arithmetic and copies ran while one was open for 15% of the time, Pallas kernels for 0%

commit v1 on v0

v1 whole, which is shorter than its diff:
```python
import functools
import math

import jax
import jax.numpy as jnp
from jax import lax
from jax.experimental import pallas as pl
from jax.experimental.pallas import tpu as pltpu
from jax.sharding import PartitionSpec as P

ITERS = 2
SUBSTEPS = 4
LATENT = 2.5
SAT_SCALE = 0.5
SAT_SLOPE = 0.2
GROWTH_RATE = 0.02
SOLUTE_WEIGHT = 0.5
LANES = 128
MESH = pl.DeviceIdType.MESH


def up(value, step):
    return -(-value // step) * step


def pair_plan(nbin):
    padded = up(nbin, 8)
    plan, row = [], 0
    for i in range(nbin):
        low = 8 * (i // 8)
        plan.append((i, low, padded - low, row))
        row += padded - low
    return plan, row


def fold_kernel(nbin, c_ref, w_ref, by_pair, folded):
    plan, rows = pair_plan(nbin)
    for start in range(0, c_ref.shape[1], LANES):
        chunk = c_ref[:, start : start + LANES].astype(jnp.float32)
        by_pair[start : start + LANES, :] = chunk.T
    for i, low, length, row in plan:
        partner = low + lax.broadcasted_iota(jnp.int32, (length, LANES), 0)
        direct = by_pair[pl.ds(nbin * i + low, length), :]
        swapped = by_pair[pl.ds(nbin * low + i, length, stride=nbin), :]
        both = jnp.where(partner > i, direct + swapped, direct)
        keep = (partner >= i) & (partner < nbin)
        folded[row : row + length, :] = jnp.where(keep, both, 0.0)
    folded[rows:, :] = jnp.zeros((folded.shape[0] - rows, LANES), jnp.float32)
    for start in range(0, folded.shape[0], LANES):
        chunk = folded[start : start + LANES, :].T
        w_ref[:, start : start + LANES] = chunk[: w_ref.shape[0]].astype(w_ref.dtype)


def fold(collision):
    nbin, pairs = collision.shape
    plan, rows = pair_plan(nbin)
    depth = up(rows, LANES)
    reach = up(max(pairs, nbin * (up(nbin, 8) - 1) + nbin), LANES)
    padded = jnp.pad(collision, ((0, LANES - nbin), (0, up(pairs, LANES) - pairs)))
    return pl.pallas_call(
        functools.partial(fold_kernel, nbin),
        out_shape=jax.ShapeDtypeStruct((up(nbin, 16), depth), jnp.bfloat16),
        in_specs=[pl.BlockSpec(memory_space=pltpu.VMEM)],
        out_specs=pl.BlockSpec(memory_space=pltpu.VMEM),
        scratch_shapes=[
            pltpu.VMEM((reach, LANES), jnp.float32),
            pltpu.VMEM((depth, LANES), jnp.float32),
        ],
        compiler_params=pltpu.CompilerParams(vmem_limit_bytes=32 * 1024 * 1024),
    )(padded)


def coupled_kernel(
    sizes, nbin,
    owner_ref, cost_ref, fields_ref, courants_ref, bins_ref, w_ref,
    fields_out, bins_out,
    owner_at, rank_at, cost_from, result_of,
    fields_mid, load_mine, load_all, excess_mine, excess_first, excess_second,
    x_low, x_high, y_low, y_high, z_low, z_high,
    face_mine, face_in, sums,
    bins_mid, moved, state, number, products,
    load_send, load_recv, excess_send, excess_recv, halo_send, halo_recv, face_send, face_recv,
):
    gx, gy, gz = sizes["gx"], sizes["gy"], sizes["gz"]
    x, y, z = lax.axis_index("gx"), lax.axis_index("gy"), lax.axis_index("gz")
    half = gx // 2
    places = 4 * gx
    cap = bins_ref.shape[0]
    cells = fields_ref.shape[2]
    columns = gy * gz
    column = y * gz + z
    last = cells - LANES
    f32 = jnp.float32
    padded = up(nbin, 8)
    excess_all = (excess_first, excess_second)

    barrier = pltpu.get_barrier_semaphore()
    for k in range(1, gx):
        pl.semaphore_signal(barrier, inc=1, device_id={"gx": lax.rem(x + k, gx)}, device_id_type=MESH)
    for name, index, count in (("gy", y, gy), ("gz", z, gz)):
        @pl.when(index > 0)
        def _():
            pl.semaphore_signal(barrier, inc=1, device_id={name: index - 1}, device_id_type=MESH)

        @pl.when(index < count - 1)
        def _():
            pl.semaphore_signal(barrier, inc=1, device_id={name: index + 1}, device_id_type=MESH)

    start = jnp.int32(0)
    count = jnp.int32(0)
    before = jnp.int32(-1)
    rank = jnp.int32(0)
    for p in range(places):
        block = (((p // 4 + half) % gx) * columns + column) * 4 + p % 4
        owner = owner_ref[block]
        rank = jnp.where(owner == before, rank + 1, 0)
        before = owner
        owner_at[p] = owner
        rank_at[p] = jnp.minimum(rank, cap - 1)
        start = start + jnp.where(owner < x, 1, 0)
        count = count + jnp.where(owner == x, 1, 0)
    first_row, valid = [], []
    ends = []
    total = jnp.int32(0)
    starts = []
    for s in range(cap):
        place = jnp.minimum(start + s, places - 1)
        tile = lax.rem(place // 4 + half, gx)
        block = (tile * columns + column) * 4 + lax.rem(place, 4)
        occupied = s < count
        valid.append(occupied)
        first_row.append((tile, lax.rem(place, 4)))
        steps = jnp.where(occupied, cost_ref[block], 0)
        starts.append(total)
        total = total + steps
        ends.append(total)
        result_of[s] = jnp.where(steps == 0, s, cap + jnp.clip(total - 1, 0, SUBSTEPS - 1))
    for t in range(SUBSTEPS):
        slot = jnp.int32(0)
        fresh = jnp.int32(0)
        for s in range(cap):
            slot = slot + jnp.where(ends[s] <= t, 1, 0)
            fresh = fresh + jnp.where((starts[s] == t) & (ends[s] > t), 1, 0)
        cost_from[t] = jnp.where(fresh > 0, jnp.minimum(slot, cap - 1), cap + t - 1)

    feature = lax.broadcasted_iota(jnp.int32, (8, bins_ref.shape[1]), 1)
    weights = jnp.where(
        feature >= 3 * nbin, 1.0, jnp.where(feature >= 2 * nbin, SOLUTE_WEIGHT, 0.0)
    ).astype(jnp.bfloat16)
    load_mine[...] = jnp.zeros(load_mine.shape, f32)
    for s in range(cap):
        summed = jnp.dot(weights, bins_ref[s], preferred_element_type=f32)
        load_mine[s : s + 1, :] = summed[0:1]
    for b in range(4):
        load_mine[8 + b : 9 + b, :] = courants_ref[b, 0:1, :]
    load_all[x] = load_mine[...]
    excess_mine[...] = jnp.zeros(excess_mine.shape, f32)

    near = lax.broadcasted_iota(jnp.int32, (1, LANES), 1) < LANES // 2

    def pack_face(ref, it):
        held = jnp.clip(count, 2, cap)
        upper = ref[held - 2, :, last:].astype(f32)
        lower = ref[held - 1, :, last:].astype(f32)
        packed = jnp.where(near, pltpu.roll(upper, LANES // 2, 1), lower)
        face_mine[it] = packed.astype(jnp.bfloat16)

    pack_face(bins_ref, 0)

    def copy(src, dst, send, recv, where):
        return pltpu.make_async_remote_copy(
            src_ref=src, dst_ref=dst, send_sem=send, recv_sem=recv,
            device_id=where, device_id_type=MESH,
        )

    def load_copies():
        return [
            copy(load_mine, load_all.at[x], load_send.at[k - 1], load_recv.at[k - 1],
                 {"gx": lax.rem(x + k, gx)})
            for k in range(1, gx)
        ]

    def excess_copies(it):
        return [
            copy(excess_mine.at[it], excess_all[it].at[x], excess_send.at[it, k - 1],
                 excess_recv.at[it, k - 1], {"gx": lax.rem(x + k, gx)})
            for k in range(1, gx)
        ]

    def halo_copies(src, it):
        out = []
        n = [0]

        def add(has_to, has_from, source, target, where):
            out.append((has_to, has_from, copy(
                source, target, halo_send.at[it, n[0]], halo_recv.at[it, n[0]], where)))
            n[0] += 1

        xu, xd = {"gx": lax.rem(x + 1, gx)}, {"gx": lax.rem(x + gx - 1, gx)}
        yu, yd = {"gy": lax.rem(y + 1, gy)}, {"gy": lax.rem(y + gy - 1, gy)}
        zu, zd = {"gz": lax.rem(z + 1, gz)}, {"gz": lax.rem(z + gz - 1, gz)}
        add(x < gx - 1, x > 0, src.at[pl.ds(2, 2), :, pl.ds(last, LANES)], x_low.at[it], xu)
        add(x > 0, x < gx - 1, src.at[pl.ds(0, 2), :, pl.ds(0, LANES)], x_high.at[it], xd)
        for a in range(2):
            add(y < gy - 1, y > 0, src.at[2 * a + 1], y_low.at[it, a], yu)
            add(y > 0, y < gy - 1, src.at[2 * a], y_high.at[it, a], yd)
        add(z < gz - 1, z > 0, src, z_low.at[it], zu)
        add(z > 0, z < gz - 1, src, z_high.at[it], zd)
        return out

    def face_copy(it):
        return copy(face_mine.at[it], face_in.at[it], face_send.at[it], face_recv.at[it],
                    {"gx": lax.rem(x + 1, gx)})

    def when_do(condition, action):
        @pl.when(condition)
        def _():
            action()

    for low, index in ((x_low, x), (y_low, y), (z_low, z)):
        def clear(low=low):
            low[...] = jnp.zeros(low.shape, f32)
        when_do(index == 0, clear)
    for high, index, size in ((x_high, x, gx), (y_high, y, gy), (z_high, z, gz)):
        def clear(high=high):
            high[...] = jnp.zeros(high.shape, f32)
        when_do(index == size - 1, clear)

    def clear_face():
        face_in[...] = jnp.zeros(face_in.shape, jnp.bfloat16)
    when_do(x == 0, clear_face)

    one = lambda flag: jnp.where(flag, 1, 0)
    pl.semaphore_wait(
        barrier, gx - 1 + one(y > 0) + one(y < gy - 1) + one(z > 0) + one(z < gz - 1)
    )

    halos = [halo_copies(fields_ref, 0), halo_copies(fields_mid, 1)]
    loads = load_copies()
    excesses = [excess_copies(it) for it in range(ITERS)]
    faces = [face_copy(it) for it in range(ITERS)]
    for has_to, has_from, message in halos[0]:
        when_do(has_to, message.start)
    for message in loads:
        message.start()
    when_do(x < gx - 1, faces[0].start)

    for message in loads:
        message.wait_recv()
    base = 4 * lax.rem(x + half, gx)
    sums[...] = jnp.zeros(sums.shape, f32)
    for q in range(6):
        place = jnp.maximum(base - 2 + q, 0)
        row = load_all[owner_at[place], pl.ds(rank_at[place], 1), :]
        if q < 2:
            row = jnp.where(base > 0, row, 0.0)
        sums[0, q : q + 1, :] = row
    sums[1, 0:2, :] = load_all[lax.rem(x + gx - 1, gx), 10:12, :]
    sums[1, 2:6, :] = load_mine[8:12, :]
    along = sums[1]
    cell = lax.broadcasted_iota(jnp.int32, (1, cells), 1)
    layer = LANES // 2

    def sum_transport(value):
        earlier = pltpu.roll(value, 2, 0)
        shifted = jnp.where(cell < layer, pltpu.roll(earlier, layer, 1), pltpu.roll(value, layer, 1))
        return value - along * (value - shifted)

    bin_sums = [sum_transport(sums[0])]
    bin_sums.append(sum_transport(bin_sums[0]))
    yc = lax.rem(cell // 8, 8)
    zc = lax.rem(cell, 8)
    kind = lax.broadcasted_iota(jnp.int32, (8, 1), 0)
    share = jnp.where(kind == 0, LATENT, jnp.where(kind == 1, -1.0, 0.0))

    def dynamics(src, dst, it):
        for has_to, has_from, message in halos[it]:
            when_do(has_from, message.wait_recv)
        for b in range(4):
            a, c = b // 2, b % 2
            g = src[b]
            west = src[b - 2, :, last:] if a else x_low[it, c]
            east = x_high[it, c] if a else src[b + 2, :, :LANES]
            south = src[b - 1] if c else y_low[it, a]
            north = y_high[it, a] if c else src[b + 1]
            wide = cells + LANES
            sides = (
                (pltpu.roll(jnp.concatenate([west, g], axis=1), layer, 1)[:, LANES:],
                 pltpu.roll(jnp.concatenate([g, east], axis=1), wide - layer, 1)[:, :cells]),
                (jnp.where(yc > 0, pltpu.roll(g, 8, 1), pltpu.roll(south, cells - 56, 1)),
                 jnp.where(yc < 7, pltpu.roll(g, cells - 8, 1), pltpu.roll(north, 56, 1))),
                (jnp.where(zc > 0, pltpu.roll(g, 1, 1), pltpu.roll(z_low[it, b], cells - 7, 1)),
                 jnp.where(zc < 7, pltpu.roll(g, cells - 1, 1), pltpu.roll(z_high[it, b], 7, 1))),
            )
            result = g
            for direction in range(3):
                low, high = sides[direction]
                component = courants_ref[b, direction : direction + 1, :]
                result = result - jnp.maximum(component, 0.0) * (g - low)
                result = result - jnp.minimum(component, 0.0) * (high - g)
            excess = result[1:2] - SAT_SCALE * jnp.exp(SAT_SLOPE * result[0:1])
            excess_mine[it, b : b + 1, :] = excess
            gained = GROWTH_RATE * excess * bin_sums[it][2 + b : 3 + b]
            dst[b] = result + share * gained
        excess_all[it][x] = excess_mine[it]
        for message in excesses[it]:
            message.start()

    bin_mass = jnp.exp(
        lax.broadcasted_iota(jnp.int32, (padded, 1), 0).astype(f32) * (math.log(8.0) / (nbin - 1))
    )
    plan, rows = pair_plan(nbin)

    def transport(src, it):
        face = face_in[it].astype(f32)
        for s in range(cap):
            tile, row = first_row[s]
            courant = load_all[tile, pl.ds(8 + row, 1), :]
            if s == 0:
                left = face
            elif s == 1:
                left = pltpu.roll(face, layer, 1)
            else:
                left = pltpu.roll(src[s - 2, :, last:].astype(f32), layer, 1)
            for lane in range(0, cells, LANES):
                u = src[s, :, lane : lane + LANES].astype(f32)
                turned = pltpu.roll(u, layer, 1)
                shifted = jnp.where(near, left, turned)
                left = turned
                moved[s, :, lane : lane + LANES] = u - courant[:, lane : lane + LANES] * (u - shifted)
            state[s, :padded, :] = moved[s, :padded, :]
            state[s, padded:, :] = moved[s, nbin : nbin + padded, :]

    def collide(t, carried):
        source = cost_from[t]
        number[...] = state[source, :padded, :]
        for m in range(0, nbin, 2):
            i, low, length, row = plan[m]
            partners = number[low:, :]
            pair = jnp.concatenate(
                [number[i : i + 1, :] * partners, number[i + 1 : i + 2, :] * partners], axis=0
            )
            products[row : row + 2 * length, :] = pair.astype(jnp.bfloat16)
        change = jnp.dot(w_ref[...], products[...], preferred_element_type=f32)[:padded]
        state[cap + t, :padded, :] = number[...] + change
        state[cap + t, padded:, :] = state[source, padded:, :] + bin_mass * change
        return carried

    def finish(dst, it):
        for s in range(cap):
            tile, row = first_row[s]
            excess = excess_all[it][tile, pl.ds(row, 1), :]
            final = result_of[s]
            growth = (GROWTH_RATE * excess) * (
                moved[s, 3 * nbin :, :] + SOLUTE_WEIGHT * moved[s, 2 * nbin : 3 * nbin, :]
            )
            moved[s, :nbin, :] = state[final, :nbin, :]
            moved[s, nbin : 2 * nbin, :] = state[final, padded : padded + nbin, :] + growth
            value = moved[s]
            if it == ITERS - 1:
                value = jnp.where(valid[s], value, 0.0)
            dst[s] = value.astype(jnp.bfloat16)

    products[rows:, :] = jnp.zeros((products.shape[0] - rows, cells), jnp.bfloat16)

    dynamics(fields_ref, fields_mid, 0)
    for has_to, has_from, message in halos[1]:
        when_do(has_to, message.start)
    when_do(x > 0, faces[0].wait_recv)
    transport(bins_ref, 0)
    lax.fori_loop(0, SUBSTEPS, collide, 0)
    for message in excesses[0]:
        message.wait_recv()
    finish(bins_mid, 0)
    pack_face(bins_mid, 1)
    when_do(x < gx - 1, faces[1].start)
    dynamics(fields_mid, fields_out, 1)
    when_do(x > 0, faces[1].wait_recv)
    transport(bins_mid, 1)
    lax.fori_loop(0, SUBSTEPS, collide, 0)
    for message in excesses[1]:
        message.wait_recv()
    finish(bins_out, 1)

    for it in range(ITERS):
        for has_to, has_from, message in halos[it]:
            when_do(has_to, message.wait_send)
        for message in excesses[it]:
            message.wait_send()
        when_do(x < gx - 1, faces[it].wait_send)
    for message in loads:
        message.wait_send()


def on_device(sizes, fields, courants, bin_moments, block_costs, block_owner, collision):
    nbin = collision.shape[0]
    folded = fold(collision)
    gx = sizes["gx"]
    cap, features, cells = bin_moments.shape
    width = fields.shape[1]
    places = 4 * gx
    padded = up(nbin, 8)
    vmem = pl.BlockSpec(memory_space=pltpu.VMEM)
    smem = pl.BlockSpec(memory_space=pltpu.SMEM)
    f32, bf16 = jnp.float32, jnp.bfloat16
    dma = pltpu.SemaphoreType.DMA
    return pl.pallas_call(
        functools.partial(coupled_kernel, sizes, nbin),
        out_shape=(
            jax.ShapeDtypeStruct(fields.shape, f32),
            jax.ShapeDtypeStruct(bin_moments.shape, bf16),
        ),
        in_specs=[smem, smem, vmem, vmem, vmem, vmem],
        out_specs=(vmem, vmem),
        scratch_shapes=[
            pltpu.SMEM((places,), jnp.int32),
            pltpu.SMEM((places,), jnp.int32),
            pltpu.SMEM((SUBSTEPS,), jnp.int32),
            pltpu.SMEM((cap,), jnp.int32),
            pltpu.VMEM(fields.shape, f32),
            pltpu.VMEM((16, cells), f32),
            pltpu.VMEM((gx, 16, cells), f32),
            pltpu.VMEM((ITERS, 8, cells), f32),
            pltpu.VMEM((gx, 8, cells), f32),
            pltpu.VMEM((gx, 8, cells), f32),
            pltpu.VMEM((ITERS, 2, width, LANES), f32),
            pltpu.VMEM((ITERS, 2, width, LANES), f32),
            pltpu.VMEM((ITERS, 2, width, cells), f32),
            pltpu.VMEM((ITERS, 2, width, cells), f32),
            pltpu.VMEM((ITERS, 4, width, cells), f32),
            pltpu.VMEM((ITERS, 4, width, cells), f32),
            pltpu.VMEM((ITERS, features, LANES), bf16),
            pltpu.VMEM((ITERS, features, LANES), bf16),
            pltpu.VMEM((2, 8, cells), f32),
            pltpu.VMEM(bin_moments.shape, bf16),
            pltpu.VMEM((cap, features, cells), f32),
            pltpu.VMEM((cap + SUBSTEPS, 2 * padded, cells), f32),
            pltpu.VMEM((padded, cells), f32),
            pltpu.VMEM((folded.shape[1], cells), bf16),
            dma((gx - 1,)),
            dma((gx - 1,)),
            dma((ITERS, gx - 1)),
            dma((ITERS, gx - 1)),
            dma((ITERS, 8)),
            dma((ITERS, 8)),
            dma((ITERS,)),
            dma((ITERS,)),
        ],
        compiler_params=pltpu.CompilerParams(
            collective_id=0, has_side_effects=True, vmem_limit_bytes=48 * 1024 * 1024
        ),
    )(block_owner, block_costs, fields, courants, bin_moments, folded)


def solution(mesh):
    parts = P(("groups", "gx", "gy", "gz"), None, None)
    return jax.shard_map(
        functools.partial(on_device, dict(mesh.shape)),
        mesh=mesh,
        in_specs=(parts, parts, parts, P("groups"), P("groups"), P()),
        out_specs=(parts, parts),
        check_vma=False,
    )
```

time: 343 us -> 27.1 us (0.08); the launches traced: 337 us -> 26.9 us
  local copies, waits for them, and re-layouts: 144 us -> 3.85 us
  other arithmetic: 78.2 us -> 0 us
  starting transfers between devices: 58.4 us -> 0 us
  matrix products: 25.7 us -> 0 us
  Pallas kernels: 0 us -> 22.3 us
  waiting for transfers between devices: 14.6 us -> 0 us
  loops' own time: 13.2 us -> 0 us
    convert_element_type x8 -> x0, local copies, waits for them, and re-layouts: 60.2 us -> none  [collide(): products = (count_rows[:, None, :] * count_rows[None, :, :]).reshape(nbin...]
    ppermute x14 -> x0, starting transfers between devices: 40.5 us -> none  [the longest x6 23.6 us: with_halo(): lax.ppermute(lax.slice_in_dim(block, block.shape[dim] - width, None, axis...]
    convert_element_type x22 -> x0, other arithmetic: 30.3 us -> none  [the longest x8 29.5 us: collide(): products = (count_rows[:, None, :] * count_rows[None, :, :]).reshape(nbin...]
    dot_general x8 -> x0, matrix products: 25.7 us -> none  [collide(): change = jnp.dot(collision, products, preferred_element_type=jnp.float32)]
    pallas_call x0 -> x2, Pallas kernels: none -> 22.3 us  [the longest x1 21.7 us: on_device(): pl.pallas_call(functools.partial(coupled_kernel, sizes, nbin), out_shape=...]
    dynamic_slice x33 -> x0, local copies, waits for them, and re-layouts: 21.9 us -> none  [the longest x30 20.5 us: on_device(): lax.map(partial(process, collision, bin_mass), (moment_state, inflows, sl...]
    all_to_all x4 -> x0, starting transfers between devices: 17.9 us -> none  [the longest x2 9.61 us: on_device(): lax.all_to_all(outgoing, 'gx', split_axis=0, concat_axis=0, tiled=True)]
    slice x76 -> x0, local copies, waits for them, and re-layouts: 16.6 us -> none  [the longest x3 4.35 us: with_halo(): lax.slice_in_dim(block, 0, width, axis=dim)]
  transfers between devices with their start and end apart: 18 -> 0, of which waited for: 5 -> 0; matrix products, arithmetic and copies ran while one was open for 15% -> 0% of each run, Pallas kernels for 0% -> 0%
where the time goes in v1:
time: 27.1 us; the launch traced here: 26.9 us
  Pallas kernels  22.3 us (82%)
  local copies, waits for them, and re-layouts  3.85 us (14%)
  between operations  0.71 us (3%)
    pallas_call x1, Pallas kernels, on_device(): pl.pallas_call(functools.partial(coupled_kernel, sizes, nbin), out_shape=...  21.7 us
    unnamed x11, local copies, waits for them, and re-layouts  2.57 us
    pad x1, local copies, waits for them, and re-layouts, fold(): jnp.pad(collision, ((0, LANES - nbin), (0, up(pairs, LANES) - pairs)))  1.28 us
    pallas_call x1, Pallas kernels, fold(): pl.pallas_call(functools.partial(fold_kernel, nbin), out_shape=jax.ShapeD...  0.62 us

profile of v1, /device:TPU:12, one launch (start us, length us, event | category | flops | bytes accessed | tf_op | source)
XLA Modules:
  0.0 26.9 jit_solution(12472080202275329100)
XLA Ops:
  0.6 0.8 %copy.8.courants_ref = f32[4,3,512]{2,1,0:T(4,128)S(1)} copy(f32[4,3,512]{2,0,1:T(4,128)} %param.7) | data formatting | bytes 49152 | tf_op args[1]
  1.4 0.0 copy-start
  1.4 0.0 copy-start.1
  1.4 0.0 copy-start.2
  1.4 0.0 copy-start.3
  1.4 1.3 %pad.4.c_ref = bf16[128,4480]{1,0:T(8,128)(2,1)S(1)} pad(bf16[66,4356]{1,0:T(8,128)(2,1)} %param.11, bf16[]{:T(256)} %constant.2.clone.1), padding=0_62x0_124 | pad | bytes 1721874 | tf_op jit(solution)/shard_map/jit(_pad)/pad | solution.py:59
  2.7 0.6 %shard_map.77.w_ref = bf16[80,2944]{1,0:T(8,128)(2,1)S(1)} custom-call(bf16[128,4480]{1,0:T(8,128)(2,1)S(1)} %pad.4.c_ref), custom_call_target="tpu_custom_call" | custom-call | tf_op jit(solution)/shard_map/pallas_call | solution.py:60
  3.3 0.0 copy-done
  3.4 0.0 copy-done.1
  3.4 0.0 copy-done.2
  3.4 0.0 copy-done.3
  3.4 21.7 %shard_map.78 = (f32[4,8,512]{2,1,0:T(8,128)S(1)}, bf16[6,264,512]{2,1,0:T(8,128)(2,1)S(1)}) custom-call(s32[64]{0:T(128)S(1)} %copy-done.2, s32[64]{0:T(128)S(1)} %copy-done.3, f32[4,8,512]{2,1,0:T(8,128)S(1)} %copy-done.1, f32[4,3,512]{2,1,0:T(4,128)S(1)} %copy.8.courants_ref, bf16[6,264,512]{2,1,0:T(8,128)(2,1)S(1)} %copy-done, ...), custom_call_target="tpu_custom_call" | custom-call | tf_op jit(solution)/shard_map/pallas_call | solution.py:407
  25.1 0.6 %copy.11 = f32[4,8,512]{2,1,0:T(8,128)} copy(f32[4,8,512]{2,1,0:T(8,128)S(1)} %get-tuple-element.4) | data formatting | bytes 131072
  25.7 1.2 %copy.12 = bf16[6,264,512]{2,1,0:T(8,128)(2,1)} copy(bf16[6,264,512]{2,1,0:T(8,128)(2,1)S(1)} %get-tuple-element.5) | data formatting | bytes 3244032
Async XLA Ops:
  1.4 2.0 %copy-start = (bf16[6,264,512]{2,1,0:T(8,128)(2,1)S(1)}, bf16[6,264,512]{2,1,0:T(8,128)(2,1)}, u32[]{:S(2)}) copy-start(bf16[6,264,512]{2,1,0:T(8,128)(2,1)} %bins_ref.1) | copy-start | bytes 4866052
  1.4 2.0 %copy-start.1 = (f32[4,8,512]{2,1,0:T(8,128)S(1)}, f32[4,8,512]{2,1,0:T(8,128)}, u32[]{:S(2)}) copy-start(f32[4,8,512]{2,1,0:T(8,128)} %fields_ref.1) | copy-start | bytes 196612
  1.4 2.0 %copy-start.2 = (s32[64]{0:T(128)S(1)}, s32[64]{0:T(128)}, u32[]{:S(2)}) copy-start(s32[64]{0:T(128)} %owner_ref.1) | copy-start | bytes 772
  1.4 2.0 %copy-start.3 = (s32[64]{0:T(128)S(1)}, s32[64]{0:T(128)}, u32[]{:S(2)}) copy-start(s32[64]{0:T(128)} %cost_ref.1) | copy-start | bytes 772

commit v2 on v1

--- a/solution.py
+++ b/solution.py
@@ -24,61 +24,57 @@
 
 
 def pair_plan(nbin):
-    padded = up(nbin, 8)
-    plan, row = [], 0
-    for i in range(nbin):
+    main = 8 * (nbin // 8)
+    plan, extra, row = [], [], 0
+    for i in range(main):
         low = 8 * (i // 8)
-        plan.append((i, low, padded - low, row))
-        row += padded - low
-    return plan, row
-
-
-def fold_kernel(nbin, c_ref, w_ref, by_pair, folded):
-    plan, rows = pair_plan(nbin)
-    for start in range(0, c_ref.shape[1], LANES):
-        chunk = c_ref[:, start : start + LANES].astype(jnp.float32)
-        by_pair[start : start + LANES, :] = chunk.T
-    for i, low, length, row in plan:
+        plan.append((i, low, row))
+        r = i - low
+        if r >= 1:
+            extra.append((row, i, main))
+        if r >= 2:
+            extra.append((row + 1, i, main + 1))
+        if r == 6 and low == 0:
+            extra += [(row + 2, main, main), (row + 3, main, main + 1), (row + 4, main + 1, main + 1)]
+        if r == 7:
+            extra += [(row + 2, low, main), (row + 3, low, main + 1), (row + 4, low + 1, main + 1)]
+        row += main - low
+    return plan, extra, row, main
+
+
+def fold(nbin, c_ref, wide, by_pair, folded, w_ref):
+    plan, extra, rows, main = pair_plan(nbin)
+    pairs = nbin * nbin
+    wide[:nbin, :pairs] = c_ref[...].astype(jnp.float32)
+    for start in range(0, wide.shape[1], LANES):
+        by_pair[start : start + LANES, :] = wide[:, start : start + LANES].T
+    for i, low, row in plan:
+        length = main - low
         partner = low + lax.broadcasted_iota(jnp.int32, (length, LANES), 0)
         direct = by_pair[pl.ds(nbin * i + low, length), :]
         swapped = by_pair[pl.ds(nbin * low + i, length, stride=nbin), :]
         both = jnp.where(partner > i, direct + swapped, direct)
-        keep = (partner >= i) & (partner < nbin)
-        folded[row : row + length, :] = jnp.where(keep, both, 0.0)
-    folded[rows:, :] = jnp.zeros((folded.shape[0] - rows, LANES), jnp.float32)
-    for start in range(0, folded.shape[0], LANES):
+        folded[row : row + length, :] = jnp.where(partner >= i, both, 0.0)
+    for row, i, j in extra:
+        value = by_pair[nbin * i + j : nbin * i + j + 1, :]
+        if i != j:
+            value = value + by_pair[nbin * j + i : nbin * j + i + 1, :]
+        folded[row : row + 1, :] = value
+    for start in range(0, rows, LANES):
         chunk = folded[start : start + LANES, :].T
         w_ref[:, start : start + LANES] = chunk[: w_ref.shape[0]].astype(w_ref.dtype)
 
 
-def fold(collision):
-    nbin, pairs = collision.shape
-    plan, rows = pair_plan(nbin)
-    depth = up(rows, LANES)
-    reach = up(max(pairs, nbin * (up(nbin, 8) - 1) + nbin), LANES)
-    padded = jnp.pad(collision, ((0, LANES - nbin), (0, up(pairs, LANES) - pairs)))
-    return pl.pallas_call(
-        functools.partial(fold_kernel, nbin),
-        out_shape=jax.ShapeDtypeStruct((up(nbin, 16), depth), jnp.bfloat16),
-        in_specs=[pl.BlockSpec(memory_space=pltpu.VMEM)],
-        out_specs=pl.BlockSpec(memory_space=pltpu.VMEM),
-        scratch_shapes=[
-            pltpu.VMEM((reach, LANES), jnp.float32),
-            pltpu.VMEM((depth, LANES), jnp.float32),
-        ],
-        compiler_params=pltpu.CompilerParams(vmem_limit_bytes=32 * 1024 * 1024),
-    )(padded)
-
-
 def coupled_kernel(
     sizes, nbin,
-    owner_ref, cost_ref, fields_ref, courants_ref, bins_ref, w_ref,
+    owner_ref, cost_ref, fields_far, courants_far, bins_far, collision_far,
     fields_out, bins_out,
     owner_at, rank_at, cost_from, result_of,
     fields_mid, load_mine, load_all, excess_mine, excess_first, excess_second,
     x_low, x_high, y_low, y_high, z_low, z_high,
     face_mine, face_in, sums,
     bins_mid, moved, state, number, products,
+    fields_ref, courants_ref, bins_ref, c_ref, wide, by_pair, folded, w_ref, local_sem,
     load_send, load_recv, excess_send, excess_recv, halo_send, halo_recv, face_send, face_recv,
 ):
     gx, gy, gz = sizes["gx"], sizes["gy"], sizes["gz"]
@@ -93,6 +89,15 @@
     f32 = jnp.float32
     padded = up(nbin, 8)
     excess_all = (excess_first, excess_second)
+
+    fetches = [
+        pltpu.make_async_copy(source, target, local_sem.at[n])
+        for n, (source, target) in enumerate((
+            (courants_far, courants_ref), (bins_far, bins_ref),
+            (fields_far, fields_ref), (collision_far, c_ref)))
+    ]
+    for fetch in fetches:
+        fetch.start()
 
     barrier = pltpu.get_barrier_semaphore()
     for k in range(1, gx):
@@ -143,11 +148,13 @@
             fresh = fresh + jnp.where((starts[s] == t) & (ends[s] > t), 1, 0)
         cost_from[t] = jnp.where(fresh > 0, jnp.minimum(slot, cap - 1), cap + t - 1)
 
-    feature = lax.broadcasted_iota(jnp.int32, (8, bins_ref.shape[1]), 1)
+    feature = lax.broadcasted_iota(jnp.int32, (8, bins_far.shape[1]), 1)
     weights = jnp.where(
         feature >= 3 * nbin, 1.0, jnp.where(feature >= 2 * nbin, SOLUTE_WEIGHT, 0.0)
     ).astype(jnp.bfloat16)
     load_mine[...] = jnp.zeros(load_mine.shape, f32)
+    fetches[0].wait()
+    fetches[1].wait()
     for s in range(cap):
         summed = jnp.dot(weights, bins_ref[s], preferred_element_type=f32)
         load_mine[s : s + 1, :] = summed[0:1]
@@ -235,7 +242,7 @@
         barrier, gx - 1 + one(y > 0) + one(y < gy - 1) + one(z > 0) + one(z < gz - 1)
     )
 
-    halos = [halo_copies(fields_ref, 0), halo_copies(fields_mid, 1)]
+    halos = [halo_copies(fields_far, 0), halo_copies(fields_mid, 1)]
     loads = load_copies()
     excesses = [excess_copies(it) for it in range(ITERS)]
     faces = [face_copy(it) for it in range(ITERS)]
@@ -244,6 +251,12 @@
     for message in loads:
         message.start()
     when_do(x < gx - 1, faces[0].start)
+
+    fetches[3].wait()
+    wide[nbin:, :] = jnp.zeros((LANES - nbin, wide.shape[1]), f32)
+    wide[:nbin, wide.shape[1] - LANES :] = jnp.zeros((nbin, LANES), f32)
+    fold(nbin, c_ref, wide, by_pair, folded, w_ref)
+    fetches[2].wait()
 
     for message in loads:
         message.wait_recv()
@@ -309,7 +322,8 @@
     bin_mass = jnp.exp(
         lax.broadcasted_iota(jnp.int32, (padded, 1), 0).astype(f32) * (math.log(8.0) / (nbin - 1))
     )
-    plan, rows = pair_plan(nbin)
+    plan, extra, rows, main = pair_plan(nbin)
+    eighth = lax.broadcasted_iota(jnp.int32, (8, 1), 0)
 
     def transport(src, it):
         face = face_in[it].astype(f32)
@@ -334,13 +348,37 @@
     def collide(t, carried):
         source = cost_from[t]
         number[...] = state[source, :padded, :]
-        for m in range(0, nbin, 2):
-            i, low, length, row = plan[m]
-            partners = number[low:, :]
-            pair = jnp.concatenate(
-                [number[i : i + 1, :] * partners, number[i + 1 : i + 2, :] * partners], axis=0
-            )
-            products[row : row + 2 * length, :] = pair.astype(jnp.bfloat16)
+        above = number[main : main + 1, :]
+        top = number[main + 1 : main + 2, :]
+        above_first = jnp.where(eighth % 2 == 0, above, top)
+        for m in range(0, main, 2):
+            pieces = []
+            for i, low, row in plan[m : m + 2]:
+                r = i - low
+                own = number[i : i + 1, :]
+                diagonal = number[low : low + 8, :]
+                left = own
+                if r == 1:
+                    diagonal = jnp.where(eighth == 0, above, diagonal)
+                elif r >= 2:
+                    diagonal = jnp.where(eighth < 2, above_first, diagonal)
+                if r == 6 and low == 0:
+                    left = jnp.where((eighth == 2) | (eighth == 3), above, own)
+                    left = jnp.where(eighth == 4, top, left)
+                if r == 7:
+                    first, second = number[low : low + 1, :], number[low + 1 : low + 2, :]
+                    left = jnp.where((eighth == 2) | (eighth == 3), first, own)
+                    left = jnp.where(eighth == 4, second, left)
+                if r == 7 or (r == 6 and low == 0):
+                    middle = (eighth >= 2) & (eighth < 4)
+                    diagonal = jnp.where(middle, above_first, diagonal)
+                    diagonal = jnp.where(eighth == 4, top, diagonal)
+                pieces.append(left * diagonal)
+                if low + 8 < main:
+                    pieces.append(own * number[low + 8 : main, :])
+            pair = jnp.concatenate(pieces, axis=0)
+            row = plan[m][2]
+            products[row : row + pair.shape[0], :] = pair.astype(jnp.bfloat16)
         change = jnp.dot(w_ref[...], products[...], preferred_element_type=f32)[:padded]
         state[cap + t, :padded, :] = number[...] + change
         state[cap + t, padded:, :] = state[source, padded:, :] + bin_mass * change
@@ -360,8 +398,6 @@
             if it == ITERS - 1:
                 value = jnp.where(valid[s], value, 0.0)
             dst[s] = value.astype(jnp.bfloat16)
-
-    products[rows:, :] = jnp.zeros((products.shape[0] - rows, cells), jnp.bfloat16)
 
     dynamics(fields_ref, fields_mid, 0)
     for has_to, has_from, message in halos[1]:
@@ -394,7 +430,9 @@
 
 def on_device(sizes, fields, courants, bin_moments, block_costs, block_owner, collision):
     nbin = collision.shape[0]
-    folded = fold(collision)
+    plan, extra, rows, main = pair_plan(nbin)
+    wide = up(nbin * nbin, LANES)
+    any_space = pl.BlockSpec(memory_space=pl.ANY)
     gx = sizes["gx"]
     cap, features, cells = bin_moments.shape
     width = fields.shape[1]
@@ -410,7 +448,7 @@
             jax.ShapeDtypeStruct(fields.shape, f32),
             jax.ShapeDtypeStruct(bin_moments.shape, bf16),
         ),
-        in_specs=[smem, smem, vmem, vmem, vmem, vmem],
+        in_specs=[smem, smem] + [any_space] * 4,
         out_specs=(vmem, vmem),
         scratch_shapes=[
             pltpu.SMEM((places,), jnp.int32),
@@ -436,7 +474,16 @@
             pltpu.VMEM((cap, features, cells), f32),
             pltpu.VMEM((cap + SUBSTEPS, 2 * padded, cells), f32),
             pltpu.VMEM((padded, cells), f32),
-            pltpu.VMEM((folded.shape[1], cells), bf16),
+            pltpu.VMEM((rows, cells), bf16),
+            pltpu.VMEM(fields.shape, f32),
+            pltpu.VMEM(courants.shape, f32),
+            pltpu.VMEM(bin_moments.shape, bf16),
+            pltpu.VMEM(collision.shape, bf16),
+            pltpu.VMEM((LANES, wide), f32),
+            pltpu.VMEM((wide, LANES), f32),
+            pltpu.VMEM((rows, LANES), f32),
+            pltpu.VMEM((up(nbin, 16), rows), bf16),
+            dma((4,)),
             dma((gx - 1,)),
             dma((gx - 1,)),
             dma((ITERS, gx - 1)),
@@ -449,7 +496,7 @@
         compiler_params=pltpu.CompilerParams(
             collective_id=0, has_side_effects=True, vmem_limit_bytes=48 * 1024 * 1024
         ),
-    )(block_owner, block_costs, fields, courants, bin_moments, folded)
+    )(block_owner, block_costs, fields, courants, bin_moments, collision)
 
 
 def solution(mesh):

time: 27.1 us -> 29.9 us (1.10)
  local copies, waits for them, and re-layouts: 3.85 us -> 7.19 us
  Pallas kernels: 22.3 us -> 21.7 us
    unnamed x11 -> x13, local copies, waits for them, and re-layouts: 2.57 us -> 7.19 us
    pad x1 -> x0, local copies, waits for them, and re-layouts: 1.28 us -> none  [fold(): jnp.pad(collision, ((0, LANES - nbin), (0, up(pairs, LANES) - pairs)))]
    pallas_call x1 -> x0, Pallas kernels: 0.62 us -> none  [fold(): pl.pallas_call(functools.partial(fold_kernel, nbin), out_shape=jax.ShapeD...]
where the time goes in v2:
time: 29.9 us; the launch traced here: 29.5 us
  Pallas kernels  21.7 us (73%)
  local copies, waits for them, and re-layouts  7.19 us (24%)
  between operations  0.65 us (2%)
    pallas_call x1, Pallas kernels, on_device(): pl.pallas_call(functools.partial(coupled_kernel, sizes, nbin), out_shape=...  21.7 us
    unnamed x13, local copies, waits for them, and re-layouts  7.19 us

profile of v2, /device:TPU:12, one launch (start us, length us, event | category | flops | bytes accessed | tf_op | source)
XLA Modules:
  0.0 29.5 jit_solution(14322903563837099210)
XLA Ops:
  0.6 0.8 %copy.8.courants_far = f32[4,3,512]{2,1,0:T(4,128)S(1)} copy(f32[4,3,512]{2,0,1:T(4,128)} %param.7) | data formatting | bytes 49152 | tf_op args[1]
  1.4 0.0 copy-start
  1.4 1.4 %copy-done = bf16[6,264,512]{2,1,0:T(8,128)(2,1)S(1)} copy-done((bf16[6,264,512]{2,1,0:T(8,128)(2,1)S(1)}, bf16[6,264,512]{2,1,0:T(8,128)(2,1)}, u32[]{:S(2)}) %copy-start) | copy-done | bytes 1622040
  2.8 0.0 copy-start.1
  2.8 1.1 %copy-done.1 = bf16[66,4356]{1,0:T(8,128)(2,1)S(1)} copy-done((bf16[66,4356]{1,0:T(8,128)(2,1)S(1)}, bf16[66,4356]{1,0:T(8,128)(2,1)}, u32[]{:S(2)}) %copy-start.1) | copy-done | bytes 575016
  3.9 0.0 copy-start.2
  3.9 0.8 %copy-done.2 = f32[4,8,512]{2,1,0:T(8,128)S(1)} copy-done((f32[4,8,512]{2,1,0:T(8,128)S(1)}, f32[4,8,512]{2,1,0:T(8,128)}, u32[]{:S(2)}) %copy-start.2) | copy-done | bytes 65560
  4.7 0.0 copy-start.3
  4.7 0.7 %copy-done.3 = s32[64]{0:T(128)S(1)} copy-done((s32[64]{0:T(128)S(1)}, s32[64]{0:T(128)}, u32[]{:S(2)}) %copy-start.3) | copy-done | bytes 280
  5.4 0.0 copy-start.4
  5.4 0.7 %copy-done.4 = s32[64]{0:T(128)S(1)} copy-done((s32[64]{0:T(128)S(1)}, s32[64]{0:T(128)}, u32[]{:S(2)}) %copy-start.4) | copy-done | bytes 280
  6.0 21.7 %shard_map.77 = (f32[4,8,512]{2,1,0:T(8,128)S(1)}, bf16[6,264,512]{2,1,0:T(8,128)(2,1)S(1)}) custom-call(s32[64]{0:T(128)S(1)} %copy-done.3, s32[64]{0:T(128)S(1)} %copy-done.4, f32[4,8,512]{2,1,0:T(8,128)S(1)} %copy-done.2, f32[4,3,512]{2,1,0:T(4,128)S(1)} %copy.8.courants_far, bf16[6,264,512]{2,1,0:T(8,128)(2,1)S(1)} %copy-done, bf16[66,4356]{1,0:T(8,128)(2,1)S(1)} %copy-done.1), custom_call_target="tpu_custom_call" | custom-call | tf_op jit(solution)/shard_map/pallas_call | solution.py:445
  27.7 0.6 %copy.11 = f32[4,8,512]{2,1,0:T(8,128)} copy(f32[4,8,512]{2,1,0:T(8,128)S(1)} %get-tuple-element.4) | data formatting | bytes 131072
  28.4 1.2 %copy.12 = bf16[6,264,512]{2,1,0:T(8,128)(2,1)} copy(bf16[6,264,512]{2,1,0:T(8,128)(2,1)S(1)} %get-tuple-element.5) | data formatting | bytes 3244032
Async XLA Ops:
  1.4 1.4 %copy-start = (bf16[6,264,512]{2,1,0:T(8,128)(2,1)S(1)}, bf16[6,264,512]{2,1,0:T(8,128)(2,1)}, u32[]{:S(2)}) copy-start(bf16[6,264,512]{2,1,0:T(8,128)(2,1)} %bins_far.1) | copy-start | bytes 4866052
  2.8 1.1 %copy-start.1 = (bf16[66,4356]{1,0:T(8,128)(2,1)S(1)}, bf16[66,4356]{1,0:T(8,128)(2,1)}, u32[]{:S(2)}) copy-start(bf16[66,4356]{1,0:T(8,128)(2,1)} %collision_far.1) | copy-start | bytes 1724980
  3.9 0.8 %copy-start.2 = (f32[4,8,512]{2,1,0:T(8,128)S(1)}, f32[4,8,512]{2,1,0:T(8,128)}, u32[]{:S(2)}) copy-start(f32[4,8,512]{2,1,0:T(8,128)} %fields_far.1) | copy-start | bytes 196612
  4.7 0.7 %copy-start.3 = (s32[64]{0:T(128)S(1)}, s32[64]{0:T(128)}, u32[]{:S(2)}) copy-start(s32[64]{0:T(128)} %owner_ref.1) | copy-start | bytes 772
  5.4 0.7 %copy-start.4 = (s32[64]{0:T(128)S(1)}, s32[64]{0:T(128)}, u32[]{:S(2)}) copy-start(s32[64]{0:T(128)} %cost_ref.1) | copy-start | bytes 772

commit v3 on v2

--- a/solution.py
+++ b/solution.py
@@ -67,9 +67,9 @@
 
 def coupled_kernel(
     sizes, nbin,
-    owner_ref, cost_ref, fields_far, courants_far, bins_far, collision_far,
+    owner_far, cost_far, fields_far, courants_far, bins_far, collision_far,
     fields_out, bins_out,
-    owner_at, rank_at, cost_from, result_of,
+    owner_ref, cost_ref, owner_at, rank_at, cost_from, result_of,
     fields_mid, load_mine, load_all, excess_mine, excess_first, excess_second,
     x_low, x_high, y_low, y_high, z_low, z_high,
     face_mine, face_in, sums,
@@ -94,10 +94,11 @@
         pltpu.make_async_copy(source, target, local_sem.at[n])
         for n, (source, target) in enumerate((
             (courants_far, courants_ref), (bins_far, bins_ref),
-            (fields_far, fields_ref), (collision_far, c_ref)))
+            (fields_far, fields_ref), (collision_far, c_ref),
+            (owner_far, owner_ref), (cost_far, cost_ref)))
     ]
-    for fetch in fetches:
-        fetch.start()
+    for n in (4, 5, 0, 1, 3, 2):
+        fetches[n].start()
 
     barrier = pltpu.get_barrier_semaphore()
     for k in range(1, gx):
@@ -111,6 +112,8 @@
         def _():
             pl.semaphore_signal(barrier, inc=1, device_id={name: index + 1}, device_id_type=MESH)
 
+    fetches[4].wait()
+    fetches[5].wait()
     start = jnp.int32(0)
     count = jnp.int32(0)
     before = jnp.int32(-1)
@@ -159,7 +162,7 @@
         summed = jnp.dot(weights, bins_ref[s], preferred_element_type=f32)
         load_mine[s : s + 1, :] = summed[0:1]
     for b in range(4):
-        load_mine[8 + b : 9 + b, :] = courants_ref[b, 0:1, :]
+        load_mine[8 + b : 9 + b, :] = courants_ref[0, b : b + 1, :]
     load_all[x] = load_mine[...]
     excess_mine[...] = jnp.zeros(excess_mine.shape, f32)
 
@@ -308,7 +311,7 @@
             result = g
             for direction in range(3):
                 low, high = sides[direction]
-                component = courants_ref[b, direction : direction + 1, :]
+                component = courants_ref[direction, b : b + 1, :]
                 result = result - jnp.maximum(component, 0.0) * (g - low)
                 result = result - jnp.minimum(component, 0.0) * (high - g)
             excess = result[1:2] - SAT_SCALE * jnp.exp(SAT_SLOPE * result[0:1])
@@ -430,16 +433,16 @@
 
 def on_device(sizes, fields, courants, bin_moments, block_costs, block_owner, collision):
     nbin = collision.shape[0]
+    courants = jnp.transpose(courants, (1, 0, 2))
     plan, extra, rows, main = pair_plan(nbin)
     wide = up(nbin * nbin, LANES)
-    any_space = pl.BlockSpec(memory_space=pl.ANY)
+    far = pl.BlockSpec(memory_space=pltpu.HBM)
     gx = sizes["gx"]
     cap, features, cells = bin_moments.shape
     width = fields.shape[1]
     places = 4 * gx
     padded = up(nbin, 8)
     vmem = pl.BlockSpec(memory_space=pltpu.VMEM)
-    smem = pl.BlockSpec(memory_space=pltpu.SMEM)
     f32, bf16 = jnp.float32, jnp.bfloat16
     dma = pltpu.SemaphoreType.DMA
     return pl.pallas_call(
@@ -448,9 +451,11 @@
             jax.ShapeDtypeStruct(fields.shape, f32),
             jax.ShapeDtypeStruct(bin_moments.shape, bf16),
         ),
-        in_specs=[smem, smem] + [any_space] * 4,
+        in_specs=[far] * 6,
         out_specs=(vmem, vmem),
         scratch_shapes=[
+            pltpu.SMEM(block_owner.shape, jnp.int32),
+            pltpu.SMEM(block_costs.shape, jnp.int32),
             pltpu.SMEM((places,), jnp.int32),
             pltpu.SMEM((places,), jnp.int32),
             pltpu.SMEM((SUBSTEPS,), jnp.int32),
@@ -483,7 +488,7 @@
             pltpu.VMEM((wide, LANES), f32),
             pltpu.VMEM((rows, LANES), f32),
             pltpu.VMEM((up(nbin, 16), rows), bf16),
-            dma((4,)),
+            dma((6,)),
             dma((gx - 1,)),
             dma((gx - 1,)),
             dma((ITERS, gx - 1)),
@@ -494,7 +499,7 @@
             dma((ITERS,)),
         ],
         compiler_params=pltpu.CompilerParams(
-            collective_id=0, has_side_effects=True, vmem_limit_bytes=48 * 1024 * 1024
+            collective_id=0, has_side_effects=True, vmem_limit_bytes=60 * 1024 * 1024
         ),
     )(block_owner, block_costs, fields, courants, bin_moments, collision)
 

time: 29.9 us -> 27.1 us (0.906)
  local copies, waits for them, and re-layouts: 7.19 us -> 4.16 us
  Pallas kernels: 21.7 us -> 22 us
    unnamed x13 -> x2, local copies, waits for them, and re-layouts: 7.19 us -> 4.16 us
    pallas_call x1, Pallas kernels: 21.7 us -> 22 us  [on_device(): pl.pallas_call(functools.partial(coupled_kernel, sizes, nbin), out_shape=...]
where the time goes in v3:
time: 27.1 us; the launch traced here: 26.8 us
  Pallas kernels  22 us (81%)
  local copies, waits for them, and re-layouts  4.16 us (15%)
  between operations  0.64 us (2%)
    pallas_call x1, Pallas kernels, on_device(): pl.pallas_call(functools.partial(coupled_kernel, sizes, nbin), out_shape=...  22 us
    unnamed x2, local copies, waits for them, and re-layouts  4.16 us

profile of v3, /device:TPU:12, one launch (start us, length us, event | category | flops | bytes accessed | tf_op | source)
XLA Modules:
  0.0 26.8 jit_solution(15666446993110295502)
XLA Ops:
  0.6 22.0 %shard_map.77 = (f32[4,8,512]{2,1,0:T(8,128)}, bf16[6,264,512]{2,1,0:T(8,128)(2,1)}) custom-call(s32[64]{0:T(128)} %owner_far.1, s32[64]{0:T(128)} %cost_far.1, f32[4,8,512]{2,1,0:T(8,128)} %fields_far.1, f32[3,4,512]{2,1,0:T(4,128)} %bitcast.1, bf16[6,264,512]{2,1,0:T(8,128)(2,1)} %bins_far.1, bf16[66,4356]{1,0:T(8,128)(2,1)} %collision_far.1), custom_call_target="tpu_custom_call" | custom-call | tf_op jit(solution)/shard_map/pallas_call | solution.py:448
  22.7 1.5 %copy.10 = f32[4,8,512]{2,1,0:T(8,128)} copy(f32[4,8,512]{2,1,0:T(8,128)} %get-tuple-element.4) | data formatting | bytes 131072
  24.1 2.7 %copy.11 = bf16[6,264,512]{2,1,0:T(8,128)(2,1)} copy(bf16[6,264,512]{2,1,0:T(8,128)(2,1)} %get-tuple-element.5) | data formatting | bytes 3244032

commit v4 on v2

--- a/solution.py
+++ b/solution.py
@@ -42,12 +42,10 @@
     return plan, extra, row, main
 
 
-def fold(nbin, c_ref, wide, by_pair, folded, w_ref):
+def fold_kernel(nbin, c_ref, w_ref, by_pair, folded):
     plan, extra, rows, main = pair_plan(nbin)
-    pairs = nbin * nbin
-    wide[:nbin, :pairs] = c_ref[...].astype(jnp.float32)
-    for start in range(0, wide.shape[1], LANES):
-        by_pair[start : start + LANES, :] = wide[:, start : start + LANES].T
+    for start in range(0, c_ref.shape[1], LANES):
+        by_pair[start : start + LANES, :] = c_ref[:, start : start + LANES].astype(jnp.float32).T
     for i, low, row in plan:
         length = main - low
         partner = low + lax.broadcasted_iota(jnp.int32, (length, LANES), 0)
@@ -65,16 +63,34 @@
         w_ref[:, start : start + LANES] = chunk[: w_ref.shape[0]].astype(w_ref.dtype)
 
 
+def fold(collision):
+    nbin, pairs = collision.shape
+    plan, extra, rows, main = pair_plan(nbin)
+    depth = rows
+    reach = up(max(pairs, nbin * (up(nbin, 8) - 1) + nbin), LANES)
+    padded = jnp.pad(collision, ((0, LANES - nbin), (0, up(pairs, LANES) - pairs)))
+    return pl.pallas_call(
+        functools.partial(fold_kernel, nbin),
+        out_shape=jax.ShapeDtypeStruct((up(nbin, 16), depth), jnp.bfloat16),
+        in_specs=[pl.BlockSpec(memory_space=pltpu.VMEM)],
+        out_specs=pl.BlockSpec(memory_space=pltpu.VMEM),
+        scratch_shapes=[
+            pltpu.VMEM((reach, LANES), jnp.float32),
+            pltpu.VMEM((depth, LANES), jnp.float32),
+        ],
+        compiler_params=pltpu.CompilerParams(vmem_limit_bytes=32 * 1024 * 1024),
+    )(padded)
+
+
 def coupled_kernel(
     sizes, nbin,
-    owner_ref, cost_ref, fields_far, courants_far, bins_far, collision_far,
+    owner_ref, cost_ref, fields_ref, courants_ref, bins_ref, w_ref,
     fields_out, bins_out,
     owner_at, rank_at, cost_from, result_of,
     fields_mid, load_mine, load_all, excess_mine, excess_first, excess_second,
     x_low, x_high, y_low, y_high, z_low, z_high,
     face_mine, face_in, sums,
     bins_mid, moved, state, number, products,
-    fields_ref, courants_ref, bins_ref, c_ref, wide, by_pair, folded, w_ref, local_sem,
     load_send, load_recv, excess_send, excess_recv, halo_send, halo_recv, face_send, face_recv,
 ):
     gx, gy, gz = sizes["gx"], sizes["gy"], sizes["gz"]
@@ -89,15 +105,6 @@
     f32 = jnp.float32
     padded = up(nbin, 8)
     excess_all = (excess_first, excess_second)
-
-    fetches = [
-        pltpu.make_async_copy(source, target, local_sem.at[n])
-        for n, (source, target) in enumerate((
-            (courants_far, courants_ref), (bins_far, bins_ref),
-            (fields_far, fields_ref), (collision_far, c_ref)))
-    ]
-    for fetch in fetches:
-        fetch.start()
 
     barrier = pltpu.get_barrier_semaphore()
     for k in range(1, gx):
@@ -148,13 +155,11 @@
             fresh = fresh + jnp.where((starts[s] == t) & (ends[s] > t), 1, 0)
         cost_from[t] = jnp.where(fresh > 0, jnp.minimum(slot, cap - 1), cap + t - 1)
 
-    feature = lax.broadcasted_iota(jnp.int32, (8, bins_far.shape[1]), 1)
+    feature = lax.broadcasted_iota(jnp.int32, (8, bins_ref.shape[1]), 1)
     weights = jnp.where(
         feature >= 3 * nbin, 1.0, jnp.where(feature >= 2 * nbin, SOLUTE_WEIGHT, 0.0)
     ).astype(jnp.bfloat16)
     load_mine[...] = jnp.zeros(load_mine.shape, f32)
-    fetches[0].wait()
-    fetches[1].wait()
     for s in range(cap):
         summed = jnp.dot(weights, bins_ref[s], preferred_element_type=f32)
         load_mine[s : s + 1, :] = summed[0:1]
@@ -242,7 +247,7 @@
         barrier, gx - 1 + one(y > 0) + one(y < gy - 1) + one(z > 0) + one(z < gz - 1)
     )
 
-    halos = [halo_copies(fields_far, 0), halo_copies(fields_mid, 1)]
+    halos = [halo_copies(fields_ref, 0), halo_copies(fields_mid, 1)]
     loads = load_copies()
     excesses = [excess_copies(it) for it in range(ITERS)]
     faces = [face_copy(it) for it in range(ITERS)]
@@ -251,12 +256,6 @@
     for message in loads:
         message.start()
     when_do(x < gx - 1, faces[0].start)
-
-    fetches[3].wait()
-    wide[nbin:, :] = jnp.zeros((LANES - nbin, wide.shape[1]), f32)
-    wide[:nbin, wide.shape[1] - LANES :] = jnp.zeros((nbin, LANES), f32)
-    fold(nbin, c_ref, wide, by_pair, folded, w_ref)
-    fetches[2].wait()
 
     for message in loads:
         message.wait_recv()
@@ -430,9 +429,7 @@
 
 def on_device(sizes, fields, courants, bin_moments, block_costs, block_owner, collision):
     nbin = collision.shape[0]
-    plan, extra, rows, main = pair_plan(nbin)
-    wide = up(nbin * nbin, LANES)
-    any_space = pl.BlockSpec(memory_space=pl.ANY)
+    folded = fold(collision)
     gx = sizes["gx"]
     cap, features, cells = bin_moments.shape
     width = fields.shape[1]
@@ -448,7 +445,7 @@
             jax.ShapeDtypeStruct(fields.shape, f32),
             jax.ShapeDtypeStruct(bin_moments.shape, bf16),
         ),
-        in_specs=[smem, smem] + [any_space] * 4,
+        in_specs=[smem, smem, vmem, vmem, vmem, vmem],
         out_specs=(vmem, vmem),
         scratch_shapes=[
             pltpu.SMEM((places,), jnp.int32),
@@ -474,16 +471,7 @@
             pltpu.VMEM((cap, features, cells), f32),
             pltpu.VMEM((cap + SUBSTEPS, 2 * padded, cells), f32),
             pltpu.VMEM((padded, cells), f32),
-            pltpu.VMEM((rows, cells), bf16),
-            pltpu.VMEM(fields.shape, f32),
-            pltpu.VMEM(courants.shape, f32),
-            pltpu.VMEM(bin_moments.shape, bf16),
-            pltpu.VMEM(collision.shape, bf16),
-            pltpu.VMEM((LANES, wide), f32),
-            pltpu.VMEM((wide, LANES), f32),
-            pltpu.VMEM((rows, LANES), f32),
-            pltpu.VMEM((up(nbin, 16), rows), bf16),
-            dma((4,)),
+            pltpu.VMEM((folded.shape[1], cells), bf16),
             dma((gx - 1,)),
             dma((gx - 1,)),
             dma((ITERS, gx - 1)),
@@ -496,7 +484,7 @@
         compiler_params=pltpu.CompilerParams(
             collective_id=0, has_side_effects=True, vmem_limit_bytes=48 * 1024 * 1024
         ),
-    )(block_owner, block_costs, fields, courants, bin_moments, collision)
+    )(block_owner, block_costs, fields, courants, bin_moments, folded)
 
 
 def solution(mesh):

time: 29.9 us -> 26.7 us (0.89)
  local copies, waits for them, and re-layouts: 7.19 us -> 3.85 us
    unnamed x13 -> x11, local copies, waits for them, and re-layouts: 7.19 us -> 2.57 us
    pad x0 -> x1, local copies, waits for them, and re-layouts: none -> 1.28 us  [fold(): jnp.pad(collision, ((0, LANES - nbin), (0, up(pairs, LANES) - pairs)))]
    pallas_call x0 -> x1, Pallas kernels: none -> 0.69 us  [fold(): pl.pallas_call(functools.partial(fold_kernel, nbin), out_shape=jax.ShapeD...]
    pallas_call x1, Pallas kernels: 21.7 us -> 21.2 us  [on_device(): pl.pallas_call(functools.partial(coupled_kernel, sizes, nbin), out_shape=...]
where the time goes in v4:
time: 26.7 us; the launch traced here: 26.4 us
  Pallas kernels  21.9 us (82%)
  local copies, waits for them, and re-layouts  3.85 us (14%)
  between operations  0.71 us (3%)
    pallas_call x1, Pallas kernels, on_device(): pl.pallas_call(functools.partial(coupled_kernel, sizes, nbin), out_shape=...  21.2 us
    unnamed x11, local copies, waits for them, and re-layouts  2.57 us
    pad x1, local copies, waits for them, and re-layouts, fold(): jnp.pad(collision, ((0, LANES - nbin), (0, up(pairs, LANES) - pairs)))  1.28 us
    pallas_call x1, Pallas kernels, fold(): pl.pallas_call(functools.partial(fold_kernel, nbin), out_shape=jax.ShapeD...  0.69 us

profile of v4, /device:TPU:12, one launch (start us, length us, event | category | flops | bytes accessed | tf_op | source)
XLA Modules:
  0.0 26.4 jit_solution(8427952695341406659)
XLA Ops:
  0.6 0.8 %copy.8.courants_ref = f32[4,3,512]{2,1,0:T(4,128)S(1)} copy(f32[4,3,512]{2,0,1:T(4,128)} %param.7) | data formatting | bytes 49152 | tf_op args[1]
  1.4 0.0 copy-start
  1.4 0.0 copy-start.1
  1.4 0.0 copy-start.2
  1.4 0.0 copy-start.3
  1.4 1.3 %pad.4.c_ref = bf16[128,4480]{1,0:T(8,128)(2,1)S(1)} pad(bf16[66,4356]{1,0:T(8,128)(2,1)} %param.11, bf16[]{:T(256)} %constant.2.clone.1), padding=0_62x0_124 | pad | bytes 1721874 | tf_op jit(solution)/shard_map/jit(_pad)/pad | solution.py:71
  2.7 0.7 %shard_map.77.w_ref = bf16[80,2304]{1,0:T(8,128)(2,1)S(1)} custom-call(bf16[128,4480]{1,0:T(8,128)(2,1)S(1)} %pad.4.c_ref), custom_call_target="tpu_custom_call" | custom-call | tf_op jit(solution)/shard_map/pallas_call | solution.py:72
  3.4 0.0 copy-done
  3.4 0.0 copy-done.1
  3.4 0.0 copy-done.2
  3.4 0.0 copy-done.3
  3.4 21.2 %shard_map.78 = (f32[4,8,512]{2,1,0:T(8,128)S(1)}, bf16[6,264,512]{2,1,0:T(8,128)(2,1)S(1)}) custom-call(s32[64]{0:T(128)S(1)} %copy-done.2, s32[64]{0:T(128)S(1)} %copy-done.3, f32[4,8,512]{2,1,0:T(8,128)S(1)} %copy-done.1, f32[4,3,512]{2,1,0:T(4,128)S(1)} %copy.8.courants_ref, bf16[6,264,512]{2,1,0:T(8,128)(2,1)S(1)} %copy-done, ...), custom_call_target="tpu_custom_call" | custom-call | tf_op jit(solution)/shard_map/pallas_call | solution.py:442
  24.7 0.6 %copy.11 = f32[4,8,512]{2,1,0:T(8,128)} copy(f32[4,8,512]{2,1,0:T(8,128)S(1)} %get-tuple-element.4) | data formatting | bytes 131072
  25.3 1.2 %copy.12 = bf16[6,264,512]{2,1,0:T(8,128)(2,1)} copy(bf16[6,264,512]{2,1,0:T(8,128)(2,1)S(1)} %get-tuple-element.5) | data formatting | bytes 3244032
Async XLA Ops:
  1.4 2.0 %copy-start = (bf16[6,264,512]{2,1,0:T(8,128)(2,1)S(1)}, bf16[6,264,512]{2,1,0:T(8,128)(2,1)}, u32[]{:S(2)}) copy-start(bf16[6,264,512]{2,1,0:T(8,128)(2,1)} %bins_ref.1) | copy-start | bytes 4866052
  1.4 2.0 %copy-start.1 = (f32[4,8,512]{2,1,0:T(8,128)S(1)}, f32[4,8,512]{2,1,0:T(8,128)}, u32[]{:S(2)}) copy-start(f32[4,8,512]{2,1,0:T(8,128)} %fields_ref.1) | copy-start | bytes 196612
  1.4 2.0 %copy-start.2 = (s32[64]{0:T(128)S(1)}, s32[64]{0:T(128)}, u32[]{:S(2)}) copy-start(s32[64]{0:T(128)} %owner_ref.1) | copy-start | bytes 772
  1.4 2.0 %copy-start.3 = (s32[64]{0:T(128)S(1)}, s32[64]{0:T(128)}, u32[]{:S(2)}) copy-start(s32[64]{0:T(128)} %cost_ref.1) | copy-start | bytes 772
